TPU v7x, 32 devices: a whole 2x2x4 slice. The times are simulated.
32 devices in a mesh: sec: 8 (over y, x, core), tile: 4 (over z).
Axes of the slice: x: 2, y: 2, z: 4, core: 2. Of those that a mesh axis runs over, the one named last changes fastest.
Arguments:
- in_plane_force: float32 [2, 16, 256, 256], P(None, 'sec', 'tile'), may hold values from -6 to 6
- stiffness: float32 [16, 256, 256], P('sec', 'tile'), may hold values from 0.5 to 2
- stiffness_z: float32 [16, 256, 256], P(None, ('tile', 'sec')), may hold values from 0.3 to 1.5
- patch_dest: int32 [8, 4, 256, 1], P('sec', 'tile'), may hold values from 0 to 7; in each aligned block of 256 rows (0 to 255, 256 to 511, ..., all dimensions but the last counted through in order) at most 64 rows name the same one
- patch_pos: int32 [8, 4, 256], P('sec', 'tile'), may hold values from 0 to 31
- patch_flow: float32 [8, 4, 256, 2, 128], P('sec', 'tile'), may hold values from -6 to 6
- patch_conf: float32 [8, 4, 256, 128], P('sec', 'tile'), may hold values from 0.2 to 1
Outputs:
- displacement: float32 [2, 16, 256, 256], P(None, None, ('tile', 'sec'))
Inputs may be any that keep to these rules, and one draw needn't show every extreme that they name: `patch_dest`: among the 256 patches of one section group and tile, at most 64 name the same owner; in some of them an owner is named exactly 64 times.
All inputs are finite; a program needn't handle non-finite values.
Results may differ from a plain program's by a relative error of at most 0.00002.
Values sent between devices are 32-bit elements; how exact they have to be, the bound alone decides.
No kernel may reach another device: no remote copies, remote signals or barrier semaphores. Data moves between devices by JAX's collectives and lax.ppermute only.
A program may use at most 64 MiB of HBM per device.

v0:
```python
import functools

import jax
import jax.numpy as jnp
from jax import lax
from jax.experimental import pallas as pl
from jax.experimental.pallas import tpu as pltpu
from jax.sharding import PartitionSpec as P

ISTEPS = 8
ZSTEPS = 8


STEP_PLANE = 0.12
STEP_CROSS = 0.15

HALO = -(-(ISTEPS - 1) // 8) * 8

VMEM = pl.BlockSpec(memory_space=pltpu.VMEM)
LIMIT = pltpu.CompilerParams(vmem_limit_bytes=8 * 1024 * 1024)
ANY = pl.BlockSpec(memory_space=pl.ANY)


def spread_kernel(layers, inner_rows, blocks, dest_ref, pos_ref, flow_ref, conf_ref, order_ref, out_ref):
    groups = out_ref.shape[0]
    count, width = conf_ref.shape
    place = pos_ref[...]
    layer = place // (inner_rows * blocks)
    inner_row = place // blocks % inner_rows
    column_block = place % blocks
    slot = (dest_ref[...] * layers + layer) * inner_rows + inner_row
    slots = groups * layers * inner_rows
    conf = conf_ref[...]
    terms = [flow_ref[pl.ds(c, count, stride=2), :] * conf for c in range(2)] + [conf]
    rest = jnp.concatenate(terms, axis=1)
    parts = []
    for _ in range(3):
        parts.append(rest.astype(jnp.bfloat16))
        rest = rest - parts[-1].astype(jnp.float32)
    numbers = lax.broadcasted_iota(jnp.int32, (slots, count), 0)
    for b in range(blocks):
        key = jnp.where(column_block == b, slot, -1)
        hit = jnp.where(numbers == key, 1.0, 0.0).astype(jnp.bfloat16)
        total = sum(jnp.dot(hit, part, preferred_element_type=jnp.float32) for part in reversed(parts))
        for o in range(groups):
            for l in range(layers):
                start = (o * layers + l) * inner_rows
                for c in range(3):
                    out_ref[o, c, l, :, b * width : (b + 1) * width] = total[
                        start : start + inner_rows, c * width : (c + 1) * width
                    ]


def shifted(blocks, lane, width):
    ahead = [pltpu.roll(x, width - 1, 1) for x in blocks]
    behind = [pltpu.roll(x, 1, 1) for x in blocks]
    zero = jnp.zeros_like(blocks[0])
    right = [jnp.where(lane == width - 1, after, own) for own, after in zip(ahead, ahead[1:] + [zero])]
    left = [jnp.where(lane == 0, before, own) for own, before in zip(behind, [zero] + behind[:-1])]
    return left, right


def plane_kernel(force_ref, stiff_ref, before_ref, after_ref, order_ref, out_ref, held, springs, keeps, pushes, even, odd):
    _, layers, rows, columns = force_ref.shape
    groups = out_ref.shape[0]
    inner_rows = rows // groups
    width = held.shape[-1]
    stride = held.shape[-2] // 8
    blocks = columns // width
    lane = lax.broadcasted_iota(jnp.int32, (8, width), 1)
    places = [(j, b) for j in range(stride) for b in range(blocks)]

    for l in range(layers):
        for c in (2, 0, 1):
            for b in range(blocks):
                span = slice(b * width, (b + 1) * width)
                held[c, l, b, :HALO] = before_ref[c, l, :, span]
                held[c, l, b, HALO : HALO + rows] = stiff_ref[l, :, span] if c == 2 else force_ref[c, l, :, span]
                held[c, l, b, HALO + rows :] = after_ref[c, l, :, span]
            for n, (j, b) in enumerate(places):
                part = STEP_PLANE * held[c, l, b, pl.ds(j, 8, stride=stride), :]
                if c == 2:
                    springs[l, n] = part
                    keeps[l, n] = 1.0 - 4.0 * part
                else:
                    pushes[l, c, n] = part

    def step(source, store):
        for l in range(layers):
            for c in range(2):
                field = [[source[l, c, j * blocks + b] for b in range(blocks)] for j in range(stride)]
                above = [[pltpu.roll(x, 1, 0) for x in field[-1]]] + field[:-1]
                below = field[1:] + [[pltpu.roll(x, 7, 0) for x in field[0]]]
                for j in range(stride):
                    left, right = shifted(field[j], lane, width)
                    for b in range(blocks):
                        n = j * blocks + b
                        near = (above[j][b] + below[j][b]) + (left[b] + right[b])
                        store(l, c, n, springs[l, n] * near + (keeps[l, n] * field[j][b] + pushes[l, c, n]))

    def to(target):
        def store(l, c, n, value):
            target[l, c, n] = value

        return store

    def to_rows(l, c, n, value):
        j, b = places[n]
        held[c, l, b, pl.ds(j, 8, stride=stride), :] = value

    def pair(_, carry):
        step(even, to(odd))
        step(odd, to(even))
        return carry

    inner = ISTEPS - 2
    source = pushes
    if inner % 2:
        step(source, to(even))
        source = even
    elif inner:
        step(source, to(odd))
        step(odd, to(even))
        source = even
    lax.fori_loop(0, (inner - 1) // 2, pair, 0)
    step(source, to_rows)
    for c in range(2):
        for l in range(layers):
            for b in range(blocks):
                for o in range(groups):
                    out_ref[o, c, l, :, b * width : (b + 1) * width] = held[
                        c, l, b, HALO + o * inner_rows : HALO + (o + 1) * inner_rows, :
                    ]


def tie_kernel(passed_ref, first_ref, out_ref):
    del passed_ref, first_ref, out_ref


def cross_kernel(moved_ref, forces_ref, stiff_ref, out_ref, result, sems):
    groups, _, layers, inner_rows, columns = moved_ref.shape
    sections = groups * layers
    width = result.shape[-1]
    blocks = columns // width
    zero = jnp.zeros((1, inner_rows, width), jnp.float32)

    def outgoing(index):
        b, c = index // 2, index % 2
        span = pl.ds(pl.multiple_of(b * width, width), width)
        return pltpu.make_async_copy(result.at[index], out_ref.at[c, :, :, span], sems.at[index])

    def one(index, carry):
        b, c = index // 2, index % 2
        span = pl.ds(pl.multiple_of(b * width, width), width)

        def channel(ref, c):
            return ref[:, c, :, :, span].reshape(sections, inner_rows, width)

        spring = STEP_CROSS * stiff_ref[:, :, span]
        weight = STEP_CROSS * channel(forces_ref, 2)
        pull = STEP_CROSS * channel(forces_ref, c)

        def step(_, field):
            rise = field - jnp.concatenate([zero, field[:-1]], axis=0)
            rise_above = jnp.concatenate([rise[1:], -field[-1:]], axis=0)
            stretch = pull - weight * rise
            stretch_above = jnp.concatenate([stretch[1:], zero], axis=0)
            return field + (spring * (rise_above - rise) + (stretch - stretch_above))

        result[index] = lax.fori_loop(0, ZSTEPS, step, channel(moved_ref, c))
        outgoing(index).start()
        return carry

    lax.fori_loop(0, 2 * blocks, one, 0)
    for index in range(2 * blocks):
        outgoing(index).wait()


def per_device(
    in_plane_force, stiffness, stiffness_z, patch_dest, patch_pos, patch_flow, patch_conf
):
    groups = lax.axis_size("sec")
    tiles = lax.axis_size("tile")
    layers, rows, columns = stiffness.shape
    inner_rows = rows // groups
    width = patch_flow.shape[-1]
    blocks = columns // width
    count = patch_pos.shape[2]
    up = [(i, i + 1) for i in range(tiles - 1)]
    down = [(j, i) for i, j in up]

    def ends(field):
        cut = field.reshape(field.shape[0], layers, rows // HALO, HALO, columns)
        return cut[:, :, :: rows // HALO - 1]

    edges = jnp.concatenate([ends(in_plane_force), ends(stiffness[None])], axis=0)
    before = lax.ppermute(edges[:, :, 1], "tile", up)
    after = lax.ppermute(edges[:, :, 0], "tile", down)
    forces = pl.pallas_call(
        functools.partial(spread_kernel, layers, inner_rows, blocks),
        out_shape=jax.ShapeDtypeStruct((groups, 3, layers, inner_rows, columns), jnp.float32),
        in_specs=[VMEM] * 4 + [ANY],
        out_specs=VMEM,
        compiler_params=LIMIT,
        cost_estimate=pl.CostEstimate(flops=6 * 256 * 256 * 384, bytes_accessed=800000, transcendentals=0),
        name="spread_patches",
    )(
        patch_dest.reshape(1, count),
        patch_pos.reshape(1, count),
        patch_flow.reshape(count * 2, width),
        patch_conf.reshape(count, width),
        edges,
    )
    moved_forces = lax.all_to_all(forces, "sec", split_axis=0, concat_axis=0, tiled=True)
    planar_shape = jax.ShapeDtypeStruct((groups, 2, layers, inner_rows, columns), jnp.float32)
    parts = (rows + 2 * HALO) // 8 * blocks
    planar = pl.pallas_call(
        plane_kernel,
        out_shape=planar_shape,
        in_specs=[VMEM] * 4 + [ANY],
        out_specs=VMEM,
        scratch_shapes=[
            pltpu.VMEM((3, layers, blocks, rows + 2 * HALO, width), jnp.float32),
            pltpu.VMEM((layers, parts, 8, width), jnp.float32),
            pltpu.VMEM((layers, parts, 8, width), jnp.float32),
            pltpu.VMEM((layers, 2, parts, 8, width), jnp.float32),
            pltpu.VMEM((layers, 2, parts, 8, width), jnp.float32),
            pltpu.VMEM((layers, 2, parts, 8, width), jnp.float32),
        ],
        compiler_params=LIMIT,
        cost_estimate=pl.CostEstimate(flops=10000000, bytes_accessed=100000000, transcendentals=0),
        name="plane_steps",
    )(in_plane_force, stiffness, before, after, forces)
    planar = pl.pallas_call(
        tie_kernel,
        out_shape=planar_shape,
        in_specs=[ANY] * 2,
        out_specs=ANY,
        input_output_aliases={0: 0},
        compiler_params=LIMIT,
        name="forces_first",
    )(planar, moved_forces)
    moved = lax.all_to_all(planar, "sec", split_axis=0, concat_axis=0, tiled=True)
    return pl.pallas_call(
        cross_kernel,
        out_shape=jax.ShapeDtypeStruct((2, groups * layers, inner_rows, columns), jnp.float32),
        in_specs=[VMEM] * 3,
        out_specs=ANY,
        scratch_shapes=[
            pltpu.VMEM((2 * blocks, groups * layers, inner_rows, width), jnp.float32),
            pltpu.SemaphoreType.DMA((2 * blocks,)),
        ],
        compiler_params=LIMIT,
        cost_estimate=pl.CostEstimate(flops=10000000, bytes_accessed=800000, transcendentals=0),
        name="cross_steps",
    )(moved, moved_forces, stiffness_z)


def solution(mesh):
    placed = (
        P(None, "sec", "tile", None),
        P("sec", "tile", None),
        P(None, ("tile", "sec"), None),
        P("sec", "tile", None, None),
        P("sec", "tile", None),
        P("sec", "tile", None, None, None),
        P("sec", "tile", None, None),
    )
    return jax.shard_map(
        per_device,
        mesh=mesh,
        in_specs=placed,
        out_specs=P(None, None, ("tile", "sec"), None),
        check_vma=False,
    )
```

profile of v0, /device:TPU:0, one launch (start us, length us, event | category | flops | bytes accessed | tf_op | source)
XLA Modules:
  0.0 32.8 jit_solution(3291674169009577970)
XLA Ops:
  0.0 0.0 copy-start.2
  0.0 0.0 copy-start.1
  0.0 0.9 %slice.12 = f32[2,2,2,8,256]{4,3,2,1,0:T(8,128)S(1)} slice(f32[2,2,8,8,256]{4,3,2,1,0:T(8,128)} %bitcast.14), slice={[0:2:1], [0:2:1], [0:8:7], [0:8:1], [0:256:1]} | slice | bytes 131072 | tf_op jit(solution)/shard_map/slice | solution.py:194
  0.9 0.0 copy-done.2
  1.0 0.0 copy-start.6
  1.0 0.0 copy-start.5
  1.0 0.1 copy-done.1
  1.1 0.6 %copy-done.6 = s32[1,1,256]{2,1,0:T(1,128)S(1)} copy-done((s32[1,1,256]{2,1,0:T(1,128)S(1)}, s32[1,1,256]{2,1,0:T(1,128)}, u32[]{:S(2)}) %copy-start.6) | copy-done | bytes 1048
  1.7 0.0 copy-done.5
  1.7 0.0 copy-start.3
  1.7 0.9 %copy-done.3 = f32[1,1,256,128]{3,2,1,0:T(8,128)S(1)} copy-done((f32[1,1,256,128]{3,2,1,0:T(8,128)S(1)}, f32[1,1,256,128]{3,2,1,0:T(8,128)}, u32[]{:S(2)}) %copy-start.3) | copy-done | bytes 131096
  2.6 1.1 %spread_patches.1.order_ref = f32[8,3,2,8,256]{4,3,2,1,0:T(8,128)} custom-call(s32[1,256]{1,0:T(1,128)S(1)} %bitcast.18, s32[1,256]{1,0:T(1,128)S(1)} %bitcast.19, f32[512,128]{1,0:T(8,128)S(1)} %bitcast.15, f32[256,128]{1,0:T(8,128)S(1)} %bitcast.17, f32[3,2,2,8,256]{4,3,2,1,0:T(8,128)S(1)} %pad_maximum_fusion.order_ref), custom_call_target="tpu_custom_call" | custom-call | flops 150994944 | bytes 800000 | tf_op jit(solution)/shard_map/spread_patches/pallas_call | solution.py:199
  3.7 0.0 copy-start
  3.7 5.3 %all-to-all-start = ((f32[8,3,2,8,256]{4,3,2,1,0:T(8,128)}), f32[8,3,2,8,256]{4,3,2,1,0:T(8,128)S(1)}, u32[]{:S(2)}, u32[]{:S(2)}) async-start(f32[8,3,2,8,256]{4,3,2,1,0:T(8,128)} %spread_patches.1.order_ref), calls=%async_computation | async-start | bytes 786432 | tf_op jit(solution)/shard_map/all_to_all | solution.py:214
  9.0 3.5 %collective-permute-start = (f32[3,2,8,256]{3,2,1,0:T(8,128)S(1)}, f32[3,2,8,256]{3,2,1,0:T(8,128)S(1)}, u32[]{:S(2)}, u32[]{:S(2)}) collective-permute-start(f32[3,2,8,256]{3,2,1,0:T(8,128)S(1)} %get-tuple-element.6), channel_id=1, source_target_pairs={{0,1},{1,2},{2,3},{4,5},{5,6},{6,7},{8,9},{9,10},{10,11},{12,13},{... | collective-permute-start | bytes 147464 | tf_op jit(solution)/shard_map/ppermute | solution.py:197
  12.5 1.3 %collective-permute-start.1 = (f32[3,2,8,256]{3,2,1,0:T(8,128)S(1)}, f32[3,2,8,256]{3,2,1,0:T(8,128)S(1)}, u32[]{:S(2)}, u32[]{:S(2)}) collective-permute-start(f32[3,2,8,256]{3,2,1,0:T(8,128)S(1)} %get-tuple-element.5), channel_id=1, source_target_pairs={{1,0},{2,1},{3,2},{5,4},{6,5},{7,6},{9,8},{10,9},{11,10},{13,12},{... | collective-permute-start | bytes 147464 | tf_op jit(solution)/shard_map/ppermute | solution.py:198
  13.8 0.4 %collective-permute-done.before_ref = f32[3,2,8,256]{3,2,1,0:T(8,128)S(1)} collective-permute-done((f32[3,2,8,256]{3,2,1,0:T(8,128)S(1)}, f32[3,2,8,256]{3,2,1,0:T(8,128)S(1)}, u32[]{:S(2)}, u32[]{:S(2)}) %collective-permute-start) | collective-permute-done | bytes 49184 | tf_op jit(solution)/shard_map/ppermute | solution.py:197
  14.3 4.3 %collective-permute-done.1.after_ref = f32[3,2,8,256]{3,2,1,0:T(8,128)S(1)} collective-permute-done((f32[3,2,8,256]{3,2,1,0:T(8,128)S(1)}, f32[3,2,8,256]{3,2,1,0:T(8,128)S(1)}, u32[]{:S(2)}, u32[]{:S(2)}) %collective-permute-start.1) | collective-permute-done | bytes 49184 | tf_op jit(solution)/shard_map/ppermute | solution.py:198
  18.5 0.0 copy-done
  18.5 1.5 %plane_steps.1.passed_ref = f32[8,2,2,8,256]{4,3,2,1,0:T(8,128)S(1)} custom-call(f32[2,2,64,256]{3,2,1,0:T(8,128)S(1)} %copy-done, f32[2,64,256]{2,1,0:T(8,128)S(1)} %copy-done.2, f32[3,2,8,256]{3,2,1,0:T(8,128)S(1)} %collective-permute-done.before_ref, f32[3,2,8,256]{3,2,1,0:T(8,128)S(1)} %collective-permute-done.1.after_ref, ...), custom_call_target="tpu_custom_call" | custom-call | flops 10000000 | bytes 100000000 | tf_op jit(solution)/shard_map/plane_steps/pallas_call | solution.py:217
  20.0 0.0 all-to-all-done.first_ref.forces_ref
  20.0 0.0 copy-start.4
  20.1 11.1 %all_to_all.10.moved_ref = f32[8,2,2,8,256]{4,3,2,1,0:T(8,128)S(1)} all-to-all(f32[8,2,2,8,256]{4,3,2,1,0:T(8,128)S(1)} %forces_first.1), channel_id=1, replica_groups=mesh['sec'=8,'tile'=4] {'sec'}, dimensions={0} | all-to-all | bytes 524288 | tf_op jit(solution)/shard_map/all_to_all | solution.py:243
  31.1 0.0 copy-done.4
  31.1 1.7 %cross_steps.1 = f32[2,16,8,256]{3,2,1,0:T(8,128)} custom-call(f32[8,2,2,8,256]{4,3,2,1,0:T(8,128)S(1)} %all_to_all.10.moved_ref, f32[8,3,2,8,256]{4,3,2,1,0:T(8,128)S(1)} %all-to-all-done.first_ref.forces_ref, f32[16,8,256]{2,1,0:T(8,128)S(1)} %copy-done.4), custom_call_target="tpu_custom_call" | custom-call | flops 10000000 | bytes 800000 | tf_op jit(solution)/shard_map/cross_steps/pallas_call | solution.py:244
  (4 shorter events, 0.0 us)
Async XLA Ops:
  0.0 0.9 %copy-start.2 = (f32[2,64,256]{2,1,0:T(8,128)S(1)}, f32[2,64,256]{2,1,0:T(8,128)}, u32[]{:S(2)}) copy-start(f32[2,64,256]{2,1,0:T(8,128)} %stiff_ref.2) | copy-start | bytes 393220
  0.0 1.1 %copy-start.1 = (f32[1,1,256,2,128]{4,3,2,1,0:T(2,128)S(1)}, f32[1,1,256,2,128]{4,3,2,1,0:T(2,128)}, u32[]{:S(2)}) copy-start(f32[1,1,256,2,128]{4,3,2,1,0:T(2,128)} %param.12) | copy-start | bytes 786436
  1.0 0.7 %copy-start.6 = (s32[1,1,256]{2,1,0:T(1,128)S(1)}, s32[1,1,256]{2,1,0:T(1,128)}, u32[]{:S(2)}) copy-start(s32[1,1,256]{2,1,0:T(1,128)} %param.11) | copy-start | bytes 3076
  1.0 0.7 %copy-start.5 = (s32[1,1,256,1]{2,3,1,0:T(1,128)S(1)}, s32[1,1,256,1]{2,3,1,0:T(1,128)}, u32[]{:S(2)}) copy-start(s32[1,1,256,1]{2,3,1,0:T(1,128)} %param.10) | copy-start | bytes 3076
  1.7 0.9 %copy-start.3 = (f32[1,1,256,128]{3,2,1,0:T(8,128)S(1)}, f32[1,1,256,128]{3,2,1,0:T(8,128)}, u32[]{:S(2)}) copy-start(f32[1,1,256,128]{3,2,1,0:T(8,128)} %param.13) | copy-start | bytes 393220
  3.7 14.8 %copy-start = (f32[2,2,64,256]{3,2,1,0:T(8,128)S(1)}, f32[2,2,64,256]{3,2,1,0:T(8,128)}, u32[]{:S(2)}) copy-start(f32[2,2,64,256]{3,2,1,0:T(8,128)} %force_ref.1) | copy-start | bytes 786436
  3.7 16.3 %all-to-all-start = ((f32[8,3,2,8,256]{4,3,2,1,0:T(8,128)}), f32[8,3,2,8,256]{4,3,2,1,0:T(8,128)S(1)}, u32[]{:S(2)}, u32[]{:S(2)}) async-start(f32[8,3,2,8,256]{4,3,2,1,0:T(8,128)} %spread_patches.1.order_ref), calls=%async_computation | async-start | bytes 786432 | tf_op jit(solution)/shard_map/all_to_all | solution.py:214
  9.0 5.2 %collective-permute-start = (f32[3,2,8,256]{3,2,1,0:T(8,128)S(1)}, f32[3,2,8,256]{3,2,1,0:T(8,128)S(1)}, u32[]{:S(2)}, u32[]{:S(2)}) collective-permute-start(f32[3,2,8,256]{3,2,1,0:T(8,128)S(1)} %get-tuple-element.6), channel_id=1, source_target_pairs={{0,1},{1,2},{2,3},{4,5},{5,6},{6,7},{8,9},{9,10},{10,11},{12,13},{... | collective-permute-start | bytes 147464 | tf_op jit(solution)/shard_map/ppermute | solution.py:197
  12.5 6.0 %collective-permute-start.1 = (f32[3,2,8,256]{3,2,1,0:T(8,128)S(1)}, f32[3,2,8,256]{3,2,1,0:T(8,128)S(1)}, u32[]{:S(2)}, u32[]{:S(2)}) collective-permute-start(f32[3,2,8,256]{3,2,1,0:T(8,128)S(1)} %get-tuple-element.5), channel_id=1, source_target_pairs={{1,0},{2,1},{3,2},{5,4},{6,5},{7,6},{9,8},{10,9},{11,10},{13,12},{... | collective-permute-start | bytes 147464 | tf_op jit(solution)/shard_map/ppermute | solution.py:198
  20.0 11.1 %copy-start.4 = (f32[16,8,256]{2,1,0:T(8,128)S(1)}, f32[16,8,256]{2,1,0:T(8,128)}, u32[]{:S(2)}) copy-start(f32[16,8,256]{2,1,0:T(8,128)} %stiff_ref.3) | copy-start | bytes 393220
where the time goes:
time: 33.1 us; the launch traced here: 32.8 us
  blocking collectives  11.1 us (34%)
  starting transfers between devices  10.1 us (31%)
  waiting for transfers between devices  4.69 us (14%)
  Pallas kernels  4.32 us (13%)
  local copies, waits for them, and re-layouts  2.55 us (8%)
    all_to_all x1, blocking collectives, per_device(): lax.all_to_all(planar, 'sec', split_axis=0, concat_axis=0, tiled=True)  11.1 us
    all_to_all x1, starting transfers between devices, per_device(): lax.all_to_all(forces, 'sec', split_axis=0, concat_axis=0, tiled=True)  5.31 us
    ppermute x1, waiting for transfers between devices, per_device(): after = lax.ppermute(edges[:, :, 0], 'tile', down)  4.25 us
    ppermute x1, starting transfers between devices, per_device(): before = lax.ppermute(edges[:, :, 1], 'tile', up)  3.48 us
    pallas_call x1, Pallas kernels, per_device(): pl.pallas_call(cross_kernel, out_shape=jax.ShapeDtypeStruct((2, groups *...  1.66 us
    unnamed x14, local copies, waits for them, and re-layouts  1.65 us
    pallas_call x1, Pallas kernels, per_device(): pl.pallas_call(plane_kernel, out_shape=planar_shape, in_specs=[VMEM] * 4...  1.52 us
    ppermute x1, starting transfers between devices, per_device(): after = lax.ppermute(edges[:, :, 0], 'tile', down)  1.29 us
  transfers between devices with their start and end apart: 3, of which 2 were waited for; matrix products, arithmetic and copies ran while one was open for 0% of the time, Pallas kernels for 5%

commit v1 on v0

--- a/solution.py
+++ b/solution.py
@@ -228,7 +228,7 @@
             pltpu.VMEM((layers, 2, parts, 8, width), jnp.float32),
         ],
         compiler_params=LIMIT,
-        cost_estimate=pl.CostEstimate(flops=10000000, bytes_accessed=100000000, transcendentals=0),
+        cost_estimate=pl.CostEstimate(flops=10**13, bytes_accessed=10**11, transcendentals=0),
         name="plane_steps",
     )(in_plane_force, stiffness, before, after, forces)
     planar = pl.pallas_call(

time: 33.1 us -> 34.3 us (1.036)
  waiting for transfers between devices: 4.69 us -> 6.81 us
  blocking collectives: 11.1 us -> 9.47 us
  Pallas kernels: 4.32 us -> 5.31 us
  local copies, waits for them, and re-layouts: 2.55 us -> 1.61 us
  starting transfers between devices: 10.1 us -> 10.6 us
    all_to_all x1, waiting for transfers between devices: 0.01 us -> 6.8 us  [per_device(): lax.all_to_all(forces, 'sec', split_axis=0, concat_axis=0, tiled=True)]
    ppermute x1, waiting for transfers between devices: 4.25 us -> 0.01 us  [per_device(): after = lax.ppermute(edges[:, :, 0], 'tile', down)]
    all_to_all x1, blocking collectives: 11.1 us -> 9.47 us  [per_device(): lax.all_to_all(planar, 'sec', split_axis=0, concat_axis=0, tiled=True)]
    ppermute x1, starting transfers between devices: 3.48 us -> 5.06 us  [per_device(): before = lax.ppermute(edges[:, :, 1], 'tile', up)]
    all_to_all x1, starting transfers between devices: 5.31 us -> 4.23 us  [per_device(): lax.all_to_all(forces, 'sec', split_axis=0, concat_axis=0, tiled=True)]
    pallas_call x1, Pallas kernels: 1.66 us -> 2.65 us  [per_device(): pl.pallas_call(cross_kernel, out_shape=jax.ShapeDtypeStruct((2, groups *...]
    unnamed x14, local copies, waits for them, and re-layouts: 1.65 us -> 0.73 us
    ppermute x1, waiting for transfers between devices: 0.43 us -> 0.01 us  [per_device(): before = lax.ppermute(edges[:, :, 1], 'tile', up)]
  transfers between devices with their start and end apart: 3 -> 3, of which waited for: 2 -> 1; matrix products, arithmetic and copies ran while one was open for 0% -> 0% of each run, Pallas kernels for 5% -> 8%
where the time goes in v1:
time: 34.3 us; the launch traced here: 33.9 us
  starting transfers between devices  10.6 us (31%)
  blocking collectives  9.47 us (28%)
  waiting for transfers between devices  6.81 us (20%)
  Pallas kernels  5.31 us (15%)
  local copies, waits for them, and re-layouts  1.61 us (5%)
    all_to_all x1, blocking collectives, per_device(): lax.all_to_all(planar, 'sec', split_axis=0, concat_axis=0, tiled=True)  9.47 us
    all_to_all x1, waiting for transfers between devices, per_device(): lax.all_to_all(forces, 'sec', split_axis=0, concat_axis=0, tiled=True)  6.8 us
    ppermute x1, starting transfers between devices, per_device(): before = lax.ppermute(edges[:, :, 1], 'tile', up)  5.06 us
    all_to_all x1, starting transfers between devices, per_device(): lax.all_to_all(forces, 'sec', split_axis=0, concat_axis=0, tiled=True)  4.23 us
    pallas_call x1, Pallas kernels, per_device(): pl.pallas_call(cross_kernel, out_shape=jax.ShapeDtypeStruct((2, groups *...  2.65 us
    pallas_call x1, Pallas kernels, per_device(): pl.pallas_call(plane_kernel, out_shape=planar_shape, in_specs=[VMEM] * 4...  1.52 us
    ppermute x1, starting transfers between devices, per_device(): after = lax.ppermute(edges[:, :, 0], 'tile', down)  1.29 us
    pallas_call x1, Pallas kernels, per_device(): pl.pallas_call(functools.partial(spread_kernel, layers, inner_rows, block...  1.14 us
  transfers between devices with their start and end apart: 3, of which 1 were waited for; matrix products, arithmetic and copies ran while one was open for 0% of the time, Pallas kernels for 8%

profile of v1, /device:TPU:0, one launch (start us, length us, event | category | flops | bytes accessed | tf_op | source)
XLA Modules:
  0.0 33.9 jit_solution(15950650510402297745)
XLA Ops:
  0.0 0.0 copy-start.4
  0.0 0.9 %slice.12 = f32[2,2,2,8,256]{4,3,2,1,0:T(8,128)S(1)} slice(f32[2,2,8,8,256]{4,3,2,1,0:T(8,128)} %bitcast.16), slice={[0:2:1], [0:2:1], [0:8:7], [0:8:1], [0:256:1]} | slice | bytes 131072 | tf_op jit(solution)/shard_map/slice | solution.py:194
  0.9 0.0 copy-start
  0.9 0.1 copy-done.4
  1.0 0.0 copy-start.1
  1.0 5.1 %collective-permute-start = (f32[3,2,8,256]{3,2,1,0:T(8,128)S(1)}, f32[3,2,8,256]{3,2,1,0:T(8,128)S(1)}, u32[]{:S(2)}, u32[]{:S(2)}) collective-permute-start(f32[3,2,8,256]{3,2,1,0:T(8,128)S(1)} %get-tuple-element.6), channel_id=1, source_target_pairs={{0,1},{1,2},{2,3},{4,5},{5,6},{6,7},{8,9},{9,10},{10,11},{12,13},{... | collective-permute-start | bytes 147464 | tf_op jit(solution)/shard_map/ppermute | solution.py:197
  6.0 1.3 %collective-permute-start.1 = (f32[3,2,8,256]{3,2,1,0:T(8,128)S(1)}, f32[3,2,8,256]{3,2,1,0:T(8,128)S(1)}, u32[]{:S(2)}, u32[]{:S(2)}) collective-permute-start(f32[3,2,8,256]{3,2,1,0:T(8,128)S(1)} %get-tuple-element.5), channel_id=1, source_target_pairs={{1,0},{2,1},{3,2},{5,4},{6,5},{7,6},{9,8},{10,9},{11,10},{13,12},{... | collective-permute-start | bytes 147464 | tf_op jit(solution)/shard_map/ppermute | solution.py:198
  7.3 0.0 copy-start.6
  7.4 0.0 copy-start.5
  7.4 0.0 copy-done
  7.4 0.0 copy-done.1
  7.4 0.6 %copy-done.6 = s32[1,1,256]{2,1,0:T(1,128)S(1)} copy-done((s32[1,1,256]{2,1,0:T(1,128)S(1)}, s32[1,1,256]{2,1,0:T(1,128)}, u32[]{:S(2)}) %copy-start.6) | copy-done | bytes 1048
  8.0 0.0 copy-done.5
  8.0 1.1 %spread_patches.1.order_ref = f32[8,3,2,8,256]{4,3,2,1,0:T(8,128)} custom-call(s32[1,256]{1,0:T(1,128)S(1)} %bitcast.18, s32[1,256]{1,0:T(1,128)S(1)} %bitcast.19, f32[512,128]{1,0:T(8,128)S(1)} %bitcast.14, f32[256,128]{1,0:T(8,128)S(1)} %bitcast.15, f32[3,2,2,8,256]{4,3,2,1,0:T(8,128)S(1)} %pad_maximum_fusion.order_ref), custom_call_target="tpu_custom_call" | custom-call | flops 150994944 | bytes 800000 | tf_op jit(solution)/shard_map/spread_patches/pallas_call | solution.py:199
  9.2 0.0 copy-start.3
  9.2 4.2 %all-to-all-start = ((f32[8,3,2,8,256]{4,3,2,1,0:T(8,128)}), f32[8,3,2,8,256]{4,3,2,1,0:T(8,128)}, u32[]{:S(2)}, u32[]{:S(2)}) async-start(f32[8,3,2,8,256]{4,3,2,1,0:T(8,128)} %spread_patches.1.order_ref), calls=%async_computation | async-start | bytes 786432 | tf_op jit(solution)/shard_map/all_to_all | solution.py:214
  13.4 0.0 collective-permute-done.before_ref
  13.4 0.0 collective-permute-done.1.after_ref
  13.4 0.0 copy-done.3
  13.5 1.5 %plane_steps.1.passed_ref = f32[8,2,2,8,256]{4,3,2,1,0:T(8,128)S(1)} custom-call(f32[2,2,64,256]{3,2,1,0:T(8,128)S(1)} %copy-done.3, f32[2,64,256]{2,1,0:T(8,128)S(1)} %copy-done.4, f32[3,2,8,256]{3,2,1,0:T(8,128)S(1)} %collective-permute-done.before_ref, f32[3,2,8,256]{3,2,1,0:T(8,128)S(1)} %collective-permute-done.1.after_ref, ...), custom_call_target="tpu_custom_call" | custom-call | flops 9999999827968 | bytes 99999997952 | tf_op jit(solution)/shard_map/plane_steps/pallas_call | solution.py:217
  15.0 6.8 %all-to-all-done.first_ref.forces_ref = f32[8,3,2,8,256]{4,3,2,1,0:T(8,128)} async-done(((f32[8,3,2,8,256]{4,3,2,1,0:T(8,128)}), f32[8,3,2,8,256]{4,3,2,1,0:T(8,128)}, u32[]{:S(2)}, u32[]{:S(2)}) %all-to-all-start) | async-done | bytes 393248 | tf_op jit(solution)/shard_map/all_to_all | solution.py:214
  21.8 0.0 copy-start.2
  21.8 9.5 %all_to_all.10.moved_ref = f32[8,2,2,8,256]{4,3,2,1,0:T(8,128)S(1)} all-to-all(f32[8,2,2,8,256]{4,3,2,1,0:T(8,128)S(1)} %forces_first.1), channel_id=1, replica_groups=mesh['sec'=8,'tile'=4] {'sec'}, dimensions={0} | all-to-all | bytes 524288 | tf_op jit(solution)/shard_map/all_to_all | solution.py:243
  31.2 0.0 copy-done.2
  31.2 2.7 %cross_steps.1 = f32[2,16,8,256]{3,2,1,0:T(8,128)} custom-call(f32[8,2,2,8,256]{4,3,2,1,0:T(8,128)S(1)} %all_to_all.10.moved_ref, f32[8,3,2,8,256]{4,3,2,1,0:T(8,128)} %all-to-all-done.first_ref.forces_ref, f32[16,8,256]{2,1,0:T(8,128)S(1)} %copy-done.2), custom_call_target="tpu_custom_call" | custom-call | flops 10000000 | bytes 800000 | tf_op jit(solution)/shard_map/cross_steps/pallas_call | solution.py:244
  (4 shorter events, 0.0 us)
Async XLA Ops:
  0.0 0.9 %copy-start.4 = (f32[2,64,256]{2,1,0:T(8,128)S(1)}, f32[2,64,256]{2,1,0:T(8,128)}, u32[]{:S(2)}) copy-start(f32[2,64,256]{2,1,0:T(8,128)} %stiff_ref.2) | copy-start | bytes 393220
  0.9 6.5 %copy-start = (f32[1,1,256,2,128]{4,3,2,1,0:T(2,128)S(1)}, f32[1,1,256,2,128]{4,3,2,1,0:T(2,128)}, u32[]{:S(2)}) copy-start(f32[1,1,256,2,128]{4,3,2,1,0:T(2,128)} %param.12) | copy-start | bytes 786436
  1.0 6.4 %copy-start.1 = (f32[1,1,256,128]{3,2,1,0:T(8,128)S(1)}, f32[1,1,256,128]{3,2,1,0:T(8,128)}, u32[]{:S(2)}) copy-start(f32[1,1,256,128]{3,2,1,0:T(8,128)} %param.13) | copy-start | bytes 393220
  1.0 12.5 %collective-permute-start = (f32[3,2,8,256]{3,2,1,0:T(8,128)S(1)}, f32[3,2,8,256]{3,2,1,0:T(8,128)S(1)}, u32[]{:S(2)}, u32[]{:S(2)}) collective-permute-start(f32[3,2,8,256]{3,2,1,0:T(8,128)S(1)} %get-tuple-element.6), channel_id=1, source_target_pairs={{0,1},{1,2},{2,3},{4,5},{5,6},{6,7},{8,9},{9,10},{10,11},{12,13},{... | collective-permute-start | bytes 147464 | tf_op jit(solution)/shard_map/ppermute | solution.py:197
  6.0 7.4 %collective-permute-start.1 = (f32[3,2,8,256]{3,2,1,0:T(8,128)S(1)}, f32[3,2,8,256]{3,2,1,0:T(8,128)S(1)}, u32[]{:S(2)}, u32[]{:S(2)}) collective-permute-start(f32[3,2,8,256]{3,2,1,0:T(8,128)S(1)} %get-tuple-element.5), channel_id=1, source_target_pairs={{1,0},{2,1},{3,2},{5,4},{6,5},{7,6},{9,8},{10,9},{11,10},{13,12},{... | collective-permute-start | bytes 147464 | tf_op jit(solution)/shard_map/ppermute | solution.py:198
  7.3 0.7 %copy-start.6 = (s32[1,1,256]{2,1,0:T(1,128)S(1)}, s32[1,1,256]{2,1,0:T(1,128)}, u32[]{:S(2)}) copy-start(s32[1,1,256]{2,1,0:T(1,128)} %param.11) | copy-start | bytes 3076
  7.4 0.7 %copy-start.5 = (s32[1,1,256,1]{2,3,1,0:T(1,128)S(1)}, s32[1,1,256,1]{2,3,1,0:T(1,128)}, u32[]{:S(2)}) copy-start(s32[1,1,256,1]{2,3,1,0:T(1,128)} %param.10) | copy-start | bytes 3076
  9.2 4.3 %copy-start.3 = (f32[2,2,64,256]{3,2,1,0:T(8,128)S(1)}, f32[2,2,64,256]{3,2,1,0:T(8,128)}, u32[]{:S(2)}) copy-start(f32[2,2,64,256]{3,2,1,0:T(8,128)} %force_ref.1) | copy-start | bytes 786436
  9.2 12.6 %all-to-all-start = ((f32[8,3,2,8,256]{4,3,2,1,0:T(8,128)}), f32[8,3,2,8,256]{4,3,2,1,0:T(8,128)}, u32[]{:S(2)}, u32[]{:S(2)}) async-start(f32[8,3,2,8,256]{4,3,2,1,0:T(8,128)} %spread_patches.1.order_ref), calls=%async_computation | async-start | bytes 786432 | tf_op jit(solution)/shard_map/all_to_all | solution.py:214
  21.8 9.5 %copy-start.2 = (f32[16,8,256]{2,1,0:T(8,128)S(1)}, f32[16,8,256]{2,1,0:T(8,128)}, u32[]{:S(2)}) copy-start(f32[16,8,256]{2,1,0:T(8,128)} %stiff_ref.3) | copy-start | bytes 393220

commit v2 on v1

--- a/solution.py
+++ b/solution.py
@@ -1,5 +1,3 @@
-import functools
-
 import jax
 import jax.numpy as jnp
 from jax import lax
@@ -21,7 +19,7 @@
 ANY = pl.BlockSpec(memory_space=pl.ANY)
 
 
-def spread_kernel(layers, inner_rows, blocks, dest_ref, pos_ref, flow_ref, conf_ref, order_ref, out_ref):
+def spread(layers, inner_rows, blocks, dest_ref, pos_ref, flow_ref, conf_ref, out_ref):
     groups = out_ref.shape[0]
     count, width = conf_ref.shape
     place = pos_ref[...]
@@ -46,7 +44,7 @@
             for l in range(layers):
                 start = (o * layers + l) * inner_rows
                 for c in range(3):
-                    out_ref[o, c, l, :, b * width : (b + 1) * width] = total[
+                    out_ref[o, 2 + c, l, :, b * width : (b + 1) * width] = total[
                         start : start + inner_rows, c * width : (c + 1) * width
                     ]
 
@@ -60,23 +58,14 @@
     return left, right
 
 
-def plane_kernel(force_ref, stiff_ref, before_ref, after_ref, order_ref, out_ref, held, springs, keeps, pushes, even, odd):
-    _, layers, rows, columns = force_ref.shape
-    groups = out_ref.shape[0]
-    inner_rows = rows // groups
-    width = held.shape[-1]
-    stride = held.shape[-2] // 8
-    blocks = columns // width
+def relax(held, springs, keeps, pushes, even, odd):
+    _, layers, blocks, total, width = held.shape
+    stride = total // 8
     lane = lax.broadcasted_iota(jnp.int32, (8, width), 1)
     places = [(j, b) for j in range(stride) for b in range(blocks)]
 
     for l in range(layers):
         for c in (2, 0, 1):
-            for b in range(blocks):
-                span = slice(b * width, (b + 1) * width)
-                held[c, l, b, :HALO] = before_ref[c, l, :, span]
-                held[c, l, b, HALO : HALO + rows] = stiff_ref[l, :, span] if c == 2 else force_ref[c, l, :, span]
-                held[c, l, b, HALO + rows :] = after_ref[c, l, :, span]
             for n, (j, b) in enumerate(places):
                 part = STEP_PLANE * held[c, l, b, pl.ds(j, 8, stride=stride), :]
                 if c == 2:
@@ -124,20 +113,65 @@
         source = even
     lax.fori_loop(0, (inner - 1) // 2, pair, 0)
     step(source, to_rows)
+
+
+def put_rows(held, out_ref, start, first, last):
+    _, layers, blocks, _, width = held.shape
+    inner_rows = out_ref.shape[3]
     for c in range(2):
         for l in range(layers):
             for b in range(blocks):
-                for o in range(groups):
-                    out_ref[o, c, l, :, b * width : (b + 1) * width] = held[
-                        c, l, b, HALO + o * inner_rows : HALO + (o + 1) * inner_rows, :
-                    ]
-
-
-def tie_kernel(passed_ref, first_ref, out_ref):
-    del passed_ref, first_ref, out_ref
-
-
-def cross_kernel(moved_ref, forces_ref, stiff_ref, out_ref, result, sems):
+                for o in range(first // inner_rows, last // inner_rows):
+                    at = start + o * inner_rows - first
+                    out_ref[o, c, l, :, b * width : (b + 1) * width] = held[c, l, b, at : at + inner_rows, :]
+
+
+def inner_kernel(dest_ref, pos_ref, flow_ref, conf_ref, force_ref, stiff_ref, order_ref, out_ref, held, *scratch):
+    layers, rows, columns = stiff_ref.shape
+    blocks, width = held.shape[2], held.shape[-1]
+    spread(layers, out_ref.shape[3], blocks, dest_ref, pos_ref, flow_ref, conf_ref, out_ref)
+    for b in range(blocks):
+        span = slice(b * width, (b + 1) * width)
+        for l in range(layers):
+            held[2, l, b] = stiff_ref[l, :, span]
+            for c in range(2):
+                held[c, l, b] = force_ref[c, l, :, span]
+    relax(held, *scratch)
+    put_rows(held, out_ref, HALO, HALO, rows - HALO)
+
+
+def ends_kernel(force_ref, stiff_ref, before_ref, after_ref, mixed_ref, out_ref, held, *scratch):
+    layers, rows, columns = stiff_ref.shape
+    blocks, width = held.shape[2], held.shape[-1]
+    edge = HALO // out_ref.shape[3]
+    for b in range(blocks):
+        span = slice(b * width, (b + 1) * width)
+        for c in range(3):
+            for l in range(layers):
+                own = stiff_ref.at[l] if c == 2 else force_ref.at[c, l]
+                held[c, l, b, :HALO] = before_ref[c, l, :, span]
+                held[c, l, b, HALO : 3 * HALO] = own[: 2 * HALO, span]
+                held[c, l, b, 3 * HALO : 5 * HALO] = own[rows - 2 * HALO :, span]
+                held[c, l, b, 5 * HALO :] = after_ref[c, l, :, span]
+    out_ref[:, 2:] = mixed_ref[:, 2:]
+    out_ref[edge:-edge, :2] = mixed_ref[edge:-edge, :2]
+    relax(held, *scratch)
+    put_rows(held, out_ref, HALO, 0, HALO)
+    put_rows(held, out_ref, 4 * HALO, rows - HALO, rows)
+
+
+def relax_scratch(layers, blocks, total, width):
+    parts = total // 8 * blocks
+    return [pltpu.VMEM((3, layers, blocks, total, width), jnp.float32)] + [
+        pltpu.VMEM((layers, parts, 8, width), jnp.float32),
+        pltpu.VMEM((layers, parts, 8, width), jnp.float32),
+        pltpu.VMEM((layers, 2, parts, 8, width), jnp.float32),
+        pltpu.VMEM((layers, 2, parts, 8, width), jnp.float32),
+        pltpu.VMEM((layers, 2, parts, 8, width), jnp.float32),
+    ]
+
+
+def cross_kernel(moved_ref, stiff_ref, out_ref, result, sems):
     groups, _, layers, inner_rows, columns = moved_ref.shape
     sections = groups * layers
     width = result.shape[-1]
@@ -153,12 +187,12 @@
         b, c = index // 2, index % 2
         span = pl.ds(pl.multiple_of(b * width, width), width)
 
-        def channel(ref, c):
-            return ref[:, c, :, :, span].reshape(sections, inner_rows, width)
+        def channel(c):
+            return moved_ref[:, c, :, :, span].reshape(sections, inner_rows, width)
 
         spring = STEP_CROSS * stiff_ref[:, :, span]
-        weight = STEP_CROSS * channel(forces_ref, 2)
-        pull = STEP_CROSS * channel(forces_ref, c)
+        weight = STEP_CROSS * channel(4)
+        pull = STEP_CROSS * channel(2 + c)
 
         def step(_, field):
             rise = field - jnp.concatenate([zero, field[:-1]], axis=0)
@@ -167,7 +201,7 @@
             stretch_above = jnp.concatenate([stretch[1:], zero], axis=0)
             return field + (spring * (rise_above - rise) + (stretch - stretch_above))
 
-        result[index] = lax.fori_loop(0, ZSTEPS, step, channel(moved_ref, c))
+        result[index] = lax.fori_loop(0, ZSTEPS, step, channel(c))
         outgoing(index).start()
         return carry
 
@@ -196,55 +230,40 @@
     edges = jnp.concatenate([ends(in_plane_force), ends(stiffness[None])], axis=0)
     before = lax.ppermute(edges[:, :, 1], "tile", up)
     after = lax.ppermute(edges[:, :, 0], "tile", down)
-    forces = pl.pallas_call(
-        functools.partial(spread_kernel, layers, inner_rows, blocks),
-        out_shape=jax.ShapeDtypeStruct((groups, 3, layers, inner_rows, columns), jnp.float32),
-        in_specs=[VMEM] * 4 + [ANY],
+    mixed_shape = jax.ShapeDtypeStruct((groups, 5, layers, inner_rows, columns), jnp.float32)
+    mixed = pl.pallas_call(
+        inner_kernel,
+        out_shape=mixed_shape,
+        in_specs=[VMEM] * 6 + [ANY],
         out_specs=VMEM,
+        scratch_shapes=relax_scratch(layers, blocks, rows, width),
         compiler_params=LIMIT,
-        cost_estimate=pl.CostEstimate(flops=6 * 256 * 256 * 384, bytes_accessed=800000, transcendentals=0),
-        name="spread_patches",
+        cost_estimate=pl.CostEstimate(flops=10**9, bytes_accessed=10**7, transcendentals=0),
+        name="spread_and_inner_rows",
     )(
         patch_dest.reshape(1, count),
         patch_pos.reshape(1, count),
         patch_flow.reshape(count * 2, width),
         patch_conf.reshape(count, width),
+        in_plane_force,
+        stiffness,
         edges,
     )
-    moved_forces = lax.all_to_all(forces, "sec", split_axis=0, concat_axis=0, tiled=True)
-    planar_shape = jax.ShapeDtypeStruct((groups, 2, layers, inner_rows, columns), jnp.float32)
-    parts = (rows + 2 * HALO) // 8 * blocks
-    planar = pl.pallas_call(
-        plane_kernel,
-        out_shape=planar_shape,
-        in_specs=[VMEM] * 4 + [ANY],
+    mixed = pl.pallas_call(
+        ends_kernel,
+        out_shape=mixed_shape,
+        in_specs=[VMEM] * 5,
         out_specs=VMEM,
-        scratch_shapes=[
-            pltpu.VMEM((3, layers, blocks, rows + 2 * HALO, width), jnp.float32),
-            pltpu.VMEM((layers, parts, 8, width), jnp.float32),
-            pltpu.VMEM((layers, parts, 8, width), jnp.float32),
-            pltpu.VMEM((layers, 2, parts, 8, width), jnp.float32),
-            pltpu.VMEM((layers, 2, parts, 8, width), jnp.float32),
-            pltpu.VMEM((layers, 2, parts, 8, width), jnp.float32),
-        ],
+        scratch_shapes=relax_scratch(layers, blocks, 6 * HALO, width),
         compiler_params=LIMIT,
-        cost_estimate=pl.CostEstimate(flops=10**13, bytes_accessed=10**11, transcendentals=0),
-        name="plane_steps",
-    )(in_plane_force, stiffness, before, after, forces)
-    planar = pl.pallas_call(
-        tie_kernel,
-        out_shape=planar_shape,
-        in_specs=[ANY] * 2,
-        out_specs=ANY,
-        input_output_aliases={0: 0},
-        compiler_params=LIMIT,
-        name="forces_first",
-    )(planar, moved_forces)
-    moved = lax.all_to_all(planar, "sec", split_axis=0, concat_axis=0, tiled=True)
+        cost_estimate=pl.CostEstimate(flops=10**7, bytes_accessed=10**6, transcendentals=0),
+        name="end_rows",
+    )(in_plane_force, stiffness, before, after, mixed)
+    moved = lax.all_to_all(mixed, "sec", split_axis=0, concat_axis=0, tiled=True)
     return pl.pallas_call(
         cross_kernel,
         out_shape=jax.ShapeDtypeStruct((2, groups * layers, inner_rows, columns), jnp.float32),
-        in_specs=[VMEM] * 3,
+        in_specs=[VMEM] * 2,
         out_specs=ANY,
         scratch_shapes=[
             pltpu.VMEM((2 * blocks, groups * layers, inner_rows, width), jnp.float32),
@@ -253,7 +272,7 @@
         compiler_params=LIMIT,
         cost_estimate=pl.CostEstimate(flops=10000000, bytes_accessed=800000, transcendentals=0),
         name="cross_steps",
-    )(moved, moved_forces, stiffness_z)
+    )(moved, stiffness_z)
 
 
 def solution(mesh):

time: 34.3 us -> 30 us (0.87)
  waiting for transfers between devices: 6.81 us -> 0.01 us
  blocking collectives: 9.47 us -> 15.2 us
  starting transfers between devices: 10.6 us -> 6.98 us
  local copies, waits for them, and re-layouts: 1.61 us -> 3.29 us
  Pallas kernels: 5.31 us -> 4.07 us
    all_to_all x1 -> x0, waiting for transfers between devices: 6.8 us -> none  [per_device(): lax.all_to_all(forces, 'sec', split_axis=0, concat_axis=0, tiled=True)]
    all_to_all x1, blocking collectives: 9.47 us -> 15.2 us  [per_device(): lax.all_to_all(mixed, 'sec', split_axis=0, concat_axis=0, tiled=True)]
    all_to_all x1 -> x0, starting transfers between devices: 4.23 us -> none  [per_device(): lax.all_to_all(forces, 'sec', split_axis=0, concat_axis=0, tiled=True)]
    pallas_call x1, Pallas kernels: 2.65 us -> 1.66 us  [per_device(): pl.pallas_call(cross_kernel, out_shape=jax.ShapeDtypeStruct((2, groups *...]
    unnamed x14, local copies, waits for them, and re-layouts: 0.73 us -> 1.62 us
    slice x2, local copies, waits for them, and re-layouts: 0.88 us -> 1.68 us  [ends(): return cut[:, :, ::rows // HALO - 1]]
    ppermute x1, starting transfers between devices: 5.06 us -> 5.56 us  [per_device(): before = lax.ppermute(edges[:, :, 1], 'tile', up)]
    pallas_call x3 -> x2, Pallas kernels: 2.66 us -> 2.42 us  [the longest x1 1.38 us: per_device(): pl.pallas_call(inner_kernel, out_shape=mixed_shape, in_specs=[VMEM] * 6 +...]
  transfers between devices with their start and end apart: 3 -> 2, of which waited for: 1 -> 0; matrix products, arithmetic and copies ran while one was open for 0% -> 0% of each run, Pallas kernels for 8% -> 5%
where the time goes in v2:
time: 30 us; the launch traced here: 29.7 us
  blocking collectives  15.2 us (51%)
  starting transfers between devices  6.98 us (23%)
  Pallas kernels  4.07 us (14%)
  local copies, waits for them, and re-layouts  3.29 us (11%)
    all_to_all x1, blocking collectives, per_device(): lax.all_to_all(mixed, 'sec', split_axis=0, concat_axis=0, tiled=True)  15.2 us
    ppermute x1, starting transfers between devices, per_device(): before = lax.ppermute(edges[:, :, 1], 'tile', up)  5.56 us
    slice x2, local copies, waits for them, and re-layouts, ends(): return cut[:, :, ::rows // HALO - 1]  1.68 us
    pallas_call x1, Pallas kernels, per_device(): pl.pallas_call(cross_kernel, out_shape=jax.ShapeDtypeStruct((2, groups *...  1.66 us
    unnamed x14, local copies, waits for them, and re-layouts  1.62 us
    ppermute x1, starting transfers between devices, per_device(): after = lax.ppermute(edges[:, :, 0], 'tile', down)  1.42 us
    pallas_call x1, Pallas kernels, per_device(): pl.pallas_call(inner_kernel, out_shape=mixed_shape, in_specs=[VMEM] * 6 +...  1.38 us
    pallas_call x1, Pallas kernels, per_device(): pl.pallas_call(ends_kernel, out_shape=mixed_shape, in_specs=[VMEM] * 5, o...  1.04 us
  transfers between devices with their start and end apart: 2, of which 0 were waited for; matrix products, arithmetic and copies ran while one was open for 0% of the time, Pallas kernels for 5%

profile of v2, /device:TPU:0, one launch (start us, length us, event | category | flops | bytes accessed | tf_op | source)
XLA Modules:
  0.0 29.7 jit_solution(18407848403845103483)
XLA Ops:
  0.0 0.8 %slice.13 = f32[1,2,2,8,256]{4,3,2,1,0:T(8,128)S(1)} slice(f32[1,2,8,8,256]{4,3,2,1,0:T(8,128)} %bitcast.15), slice={[0:1:1], [0:2:1], [0:8:7], [0:8:1], [0:256:1]} | slice | bytes 65536 | tf_op jit(solution)/shard_map/slice | solution.py:228
  0.8 0.0 copy-start
  0.8 0.9 %slice.12 = f32[2,2,2,8,256]{4,3,2,1,0:T(8,128)S(1)} slice(f32[2,2,8,8,256]{4,3,2,1,0:T(8,128)} %bitcast.14), slice={[0:2:1], [0:2:1], [0:8:7], [0:8:1], [0:256:1]} | slice | bytes 131072 | tf_op jit(solution)/shard_map/slice | solution.py:228
  1.7 0.0 copy-start.4
  1.7 0.0 copy-start.1
  1.7 1.4 %collective-permute-start.1 = (f32[3,2,8,256]{3,2,1,0:T(8,128)S(1)}, f32[3,2,8,256]{3,2,1,0:T(8,128)S(1)}, u32[]{:S(2)}, u32[]{:S(2)}) collective-permute-start(f32[3,2,8,256]{3,2,1,0:T(8,128)S(1)} %get-tuple-element.5), channel_id=1, source_target_pairs={{1,0},{2,1},{3,2},{5,4},{6,5},{7,6},{9,8},{10,9},{11,10},{13,12},{... | collective-permute-start | bytes 147464 | tf_op jit(solution)/shard_map/ppermute | solution.py:232
  3.1 5.6 %collective-permute-start = (f32[3,2,8,256]{3,2,1,0:T(8,128)S(1)}, f32[3,2,8,256]{3,2,1,0:T(8,128)S(1)}, u32[]{:S(2)}, u32[]{:S(2)}) collective-permute-start(f32[3,2,8,256]{3,2,1,0:T(8,128)S(1)} %get-tuple-element.6), channel_id=1, source_target_pairs={{0,1},{1,2},{2,3},{4,5},{5,6},{6,7},{8,9},{9,10},{10,11},{12,13},{... | collective-permute-start | bytes 147464 | tf_op jit(solution)/shard_map/ppermute | solution.py:231
  8.7 0.0 copy-start.6
  8.7 0.0 copy-start.5
  8.7 0.0 copy-done
  8.8 0.0 copy-done.4
  8.8 0.0 copy-done.1
  8.8 0.6 %copy-done.6 = s32[1,1,256]{2,1,0:T(1,128)S(1)} copy-done((s32[1,1,256]{2,1,0:T(1,128)S(1)}, s32[1,1,256]{2,1,0:T(1,128)}, u32[]{:S(2)}) %copy-start.6) | copy-done | bytes 1048
  9.4 0.0 copy-done.5
  9.4 0.0 copy-start.3
  9.4 0.9 %copy-done.3 = f32[1,1,256,2,128]{4,3,2,1,0:T(2,128)S(1)} copy-done((f32[1,1,256,2,128]{4,3,2,1,0:T(2,128)S(1)}, f32[1,1,256,2,128]{4,3,2,1,0:T(2,128)}, u32[]{:S(2)}) %copy-start.3) | copy-done | bytes 262168
  10.4 1.4 %spread_and_inner_rows.1.mixed_ref = f32[8,5,2,8,256]{4,3,2,1,0:T(8,128)S(1)} custom-call(s32[1,256]{1,0:T(1,128)S(1)} %bitcast.18, s32[1,256]{1,0:T(1,128)S(1)} %bitcast.19, f32[512,128]{1,0:T(8,128)S(1)} %bitcast.16, f32[256,128]{1,0:T(8,128)S(1)} %bitcast.17, f32[2,2,64,256]{3,2,1,0:T(8,128)S(1)} %copy-done, f32[2,64,256]{2,1,0:T(8,128)S(1)} %copy-done.1, ...), custom_call_target="tpu_custom_call" | custom-call | flops 1000000000 | bytes 10000000 | tf_op jit(solution)/shard_map/spread_and_inner_rows/pallas_call | solution.py:234
  11.7 0.0 collective-permute-done.1.after_ref
  11.8 0.0 collective-permute-done.before_ref
  11.8 1.0 %end_rows.1 = f32[8,5,2,8,256]{4,3,2,1,0:T(8,128)S(1)} custom-call(f32[2,2,64,256]{3,2,1,0:T(8,128)S(1)} %copy-done, f32[2,64,256]{2,1,0:T(8,128)S(1)} %copy-done.1, f32[3,2,8,256]{3,2,1,0:T(8,128)S(1)} %collective-permute-done.before_ref, f32[3,2,8,256]{3,2,1,0:T(8,128)S(1)} %collective-permute-done.1.after_ref, ...), custom_call_target="tpu_custom_call" | custom-call | flops 10000000 | bytes 1000000 | tf_op jit(solution)/shard_map/end_rows/pallas_call | solution.py:252
  12.8 0.0 copy-start.2
  12.8 15.2 %all_to_all.5.moved_ref = f32[8,5,2,8,256]{4,3,2,1,0:T(8,128)S(1)} all-to-all(f32[8,5,2,8,256]{4,3,2,1,0:T(8,128)S(1)} %end_rows.1), channel_id=1, replica_groups=mesh['sec'=8,'tile'=4] {'sec'}, dimensions={0} | all-to-all | bytes 1310720 | tf_op jit(solution)/shard_map/all_to_all | solution.py:262
  28.1 0.0 copy-done.2
  28.1 1.7 %cross_steps.1 = f32[2,16,8,256]{3,2,1,0:T(8,128)} custom-call(f32[8,5,2,8,256]{4,3,2,1,0:T(8,128)S(1)} %all_to_all.5.moved_ref, f32[16,8,256]{2,1,0:T(8,128)S(1)} %copy-done.2), custom_call_target="tpu_custom_call" | custom-call | flops 10000000 | bytes 800000 | tf_op jit(solution)/shard_map/cross_steps/pallas_call | solution.py:263
  (2 shorter events, 0.0 us)
Async XLA Ops:
  0.8 8.0 %copy-start = (f32[2,2,64,256]{3,2,1,0:T(8,128)S(1)}, f32[2,2,64,256]{3,2,1,0:T(8,128)}, u32[]{:S(2)}) copy-start(f32[2,2,64,256]{3,2,1,0:T(8,128)} %force_ref.3) | copy-start | bytes 786436
  1.7 7.1 %copy-start.4 = (f32[1,1,256,128]{3,2,1,0:T(8,128)S(1)}, f32[1,1,256,128]{3,2,1,0:T(8,128)}, u32[]{:S(2)}) copy-start(f32[1,1,256,128]{3,2,1,0:T(8,128)} %param.13) | copy-start | bytes 393220
  1.7 7.1 %copy-start.1 = (f32[2,64,256]{2,1,0:T(8,128)S(1)}, f32[2,64,256]{2,1,0:T(8,128)}, u32[]{:S(2)}) copy-start(f32[2,64,256]{2,1,0:T(8,128)} %stiff_ref.4) | copy-start | bytes 393220
  1.7 10.0 %collective-permute-start.1 = (f32[3,2,8,256]{3,2,1,0:T(8,128)S(1)}, f32[3,2,8,256]{3,2,1,0:T(8,128)S(1)}, u32[]{:S(2)}, u32[]{:S(2)}) collective-permute-start(f32[3,2,8,256]{3,2,1,0:T(8,128)S(1)} %get-tuple-element.5), channel_id=1, source_target_pairs={{1,0},{2,1},{3,2},{5,4},{6,5},{7,6},{9,8},{10,9},{11,10},{13,12},{... | collective-permute-start | bytes 147464 | tf_op jit(solution)/shard_map/ppermute | solution.py:232
  3.1 8.6 %collective-permute-start = (f32[3,2,8,256]{3,2,1,0:T(8,128)S(1)}, f32[3,2,8,256]{3,2,1,0:T(8,128)S(1)}, u32[]{:S(2)}, u32[]{:S(2)}) collective-permute-start(f32[3,2,8,256]{3,2,1,0:T(8,128)S(1)} %get-tuple-element.6), channel_id=1, source_target_pairs={{0,1},{1,2},{2,3},{4,5},{5,6},{6,7},{8,9},{9,10},{10,11},{12,13},{... | collective-permute-start | bytes 147464 | tf_op jit(solution)/shard_map/ppermute | solution.py:231
  8.7 0.7 %copy-start.6 = (s32[1,1,256]{2,1,0:T(1,128)S(1)}, s32[1,1,256]{2,1,0:T(1,128)}, u32[]{:S(2)}) copy-start(s32[1,1,256]{2,1,0:T(1,128)} %param.11) | copy-start | bytes 3076
  8.7 0.7 %copy-start.5 = (s32[1,1,256,1]{2,3,1,0:T(1,128)S(1)}, s32[1,1,256,1]{2,3,1,0:T(1,128)}, u32[]{:S(2)}) copy-start(s32[1,1,256,1]{2,3,1,0:T(1,128)} %param.10) | copy-start | bytes 3076
  9.4 0.9 %copy-start.3 = (f32[1,1,256,2,128]{4,3,2,1,0:T(2,128)S(1)}, f32[1,1,256,2,128]{4,3,2,1,0:T(2,128)}, u32[]{:S(2)}) copy-start(f32[1,1,256,2,128]{4,3,2,1,0:T(2,128)} %param.12) | copy-start | bytes 786436
  12.8 15.3 %copy-start.2 = (f32[16,8,256]{2,1,0:T(8,128)S(1)}, f32[16,8,256]{2,1,0:T(8,128)}, u32[]{:S(2)}) copy-start(f32[16,8,256]{2,1,0:T(8,128)} %stiff_ref.5) | copy-start | bytes 393220

commit v3 on v2

--- a/solution.py
+++ b/solution.py
@@ -97,21 +97,11 @@
         j, b = places[n]
         held[c, l, b, pl.ds(j, 8, stride=stride), :] = value
 
-    def pair(_, carry):
-        step(even, to(odd))
-        step(odd, to(even))
-        return carry
-
-    inner = ISTEPS - 2
     source = pushes
-    if inner % 2:
-        step(source, to(even))
-        source = even
-    elif inner:
-        step(source, to(odd))
-        step(odd, to(even))
-        source = even
-    lax.fori_loop(0, (inner - 1) // 2, pair, 0)
+    for n in range(ISTEPS - 2):
+        target = odd if n % 2 else even
+        step(source, to(target))
+        source = target
     step(source, to_rows)
 
 
@@ -126,7 +116,7 @@
                     out_ref[o, c, l, :, b * width : (b + 1) * width] = held[c, l, b, at : at + inner_rows, :]
 
 
-def inner_kernel(dest_ref, pos_ref, flow_ref, conf_ref, force_ref, stiff_ref, order_ref, out_ref, held, *scratch):
+def inner_kernel(dest_ref, pos_ref, flow_ref, conf_ref, force_ref, stiff_ref, out_ref, held, *scratch):
     layers, rows, columns = stiff_ref.shape
     blocks, width = held.shape[2], held.shape[-1]
     spread(layers, out_ref.shape[3], blocks, dest_ref, pos_ref, flow_ref, conf_ref, out_ref)
@@ -201,7 +191,7 @@
             stretch_above = jnp.concatenate([stretch[1:], zero], axis=0)
             return field + (spring * (rise_above - rise) + (stretch - stretch_above))
 
-        result[index] = lax.fori_loop(0, ZSTEPS, step, channel(c))
+        result[index] = lax.fori_loop(0, ZSTEPS, step, channel(c), unroll=True)
         outgoing(index).start()
         return carry
 
@@ -227,14 +217,14 @@
         cut = field.reshape(field.shape[0], layers, rows // HALO, HALO, columns)
         return cut[:, :, :: rows // HALO - 1]
 
-    edges = jnp.concatenate([ends(in_plane_force), ends(stiffness[None])], axis=0)
+    edges = jnp.pad(ends(in_plane_force), ((0, 1),) + ((0, 0),) * 4) + jnp.pad(ends(stiffness[None]), ((2, 0),) + ((0, 0),) * 4)
     before = lax.ppermute(edges[:, :, 1], "tile", up)
     after = lax.ppermute(edges[:, :, 0], "tile", down)
     mixed_shape = jax.ShapeDtypeStruct((groups, 5, layers, inner_rows, columns), jnp.float32)
     mixed = pl.pallas_call(
         inner_kernel,
         out_shape=mixed_shape,
-        in_specs=[VMEM] * 6 + [ANY],
+        in_specs=[VMEM] * 6,
         out_specs=VMEM,
         scratch_shapes=relax_scratch(layers, blocks, rows, width),
         compiler_params=LIMIT,
@@ -247,7 +237,6 @@
         patch_conf.reshape(count, width),
         in_plane_force,
         stiffness,
-        edges,
     )
     mixed = pl.pallas_call(
         ends_kernel,

time: 30 us -> 30.3 us (1.010)
  other arithmetic: 0.02 us -> 0.82 us
  Pallas kernels: 4.07 us -> 3.49 us
    unnamed x14, local copies, waits for them, and re-layouts: 1.62 us -> 3.48 us
    slice x2 -> x0, local copies, waits for them, and re-layouts: 1.68 us -> none  [ends(): return cut[:, :, ::rows // HALO - 1]]
    squeeze x1, other arithmetic: 0.01 us -> 0.82 us  [per_device(): after = lax.ppermute(edges[:, :, 0], 'tile', down)]
  transfers between devices with their start and end apart: 2 -> 2, of which waited for: 0 -> 0; matrix products, arithmetic and copies ran while one was open for 0% -> 0% of each run, Pallas kernels for 5% -> 4%
where the time goes in v3:
time: 30.3 us; the launch traced here: 30 us
  blocking collectives  15.2 us (50%)
  starting transfers between devices  6.85 us (23%)
  Pallas kernels  3.49 us (12%)
  local copies, waits for them, and re-layouts  3.48 us (11%)
  other arithmetic  0.82 us (3%)
    all_to_all x1, blocking collectives, per_device(): lax.all_to_all(mixed, 'sec', split_axis=0, concat_axis=0, tiled=True)  15.2 us
    ppermute x1, starting transfers between devices, per_device(): before = lax.ppermute(edges[:, :, 1], 'tile', up)  5.56 us
    unnamed x14, local copies, waits for them, and re-layouts  3.48 us
    pallas_call x1, Pallas kernels, per_device(): pl.pallas_call(cross_kernel, out_shape=jax.ShapeDtypeStruct((2, groups *...  1.49 us
    ppermute x1, starting transfers between devices, per_device(): after = lax.ppermute(edges[:, :, 0], 'tile', down)  1.29 us
    pallas_call x1, Pallas kernels, per_device(): pl.pallas_call(inner_kernel, out_shape=mixed_shape, in_specs=[VMEM] * 6,...  1.19 us
    squeeze x1, other arithmetic, per_device(): after = lax.ppermute(edges[:, :, 0], 'tile', down)  0.82 us
    pallas_call x1, Pallas kernels, per_device(): pl.pallas_call(ends_kernel, out_shape=mixed_shape, in_specs=[VMEM] * 5, o...  0.82 us
  transfers between devices with their start and end apart: 2, of which 0 were waited for; matrix products, arithmetic and copies ran while one was open for 0% of the time, Pallas kernels for 4%

profile of v3, /device:TPU:0, one launch (start us, length us, event | category | flops | bytes accessed | tf_op | source)
XLA Modules:
  0.0 30.0 jit_solution(3769477092928820744)
XLA Ops:
  0.0 0.0 copy-start.1
  0.0 0.8 %fusion.2 = (f32[3,2,8,256]{3,2,1,0:T(8,128)S(1)}, f32[3,2,8,256]{3,2,1,0:T(8,128)S(1)}) fusion(f32[2,2,8,8,256]{4,3,2,1,0:T(8,128)} %bitcast.10, f32[1,2,8,8,256]{4,3,2,1,0:T(8,128)} %bitcast.11), kind=kLoop, calls=%fused_computation.5 | loop fusion | flops 24576 | bytes 196608 | tf_op jit(solution)/shard_map/squeeze | solution.py:222
  0.8 1.3 %collective-permute-start.1 = (f32[3,2,8,256]{3,2,1,0:T(8,128)S(1)}, f32[3,2,8,256]{3,2,1,0:T(8,128)S(1)}, u32[]{:S(2)}, u32[]{:S(2)}) collective-permute-start(f32[3,2,8,256]{3,2,1,0:T(8,128)S(1)} %get-tuple-element.5), channel_id=1, source_target_pairs={{1,0},{2,1},{3,2},{5,4},{6,5},{7,6},{9,8},{10,9},{11,10},{13,12},{... | collective-permute-start | bytes 147464 | tf_op jit(solution)/shard_map/ppermute | solution.py:222
  2.1 5.6 %collective-permute-start = (f32[3,2,8,256]{3,2,1,0:T(8,128)S(1)}, f32[3,2,8,256]{3,2,1,0:T(8,128)S(1)}, u32[]{:S(2)}, u32[]{:S(2)}) collective-permute-start(f32[3,2,8,256]{3,2,1,0:T(8,128)S(1)} %get-tuple-element.6), channel_id=1, source_target_pairs={{0,1},{1,2},{2,3},{4,5},{5,6},{6,7},{8,9},{9,10},{10,11},{12,13},{... | collective-permute-start | bytes 147464 | tf_op jit(solution)/shard_map/ppermute | solution.py:221
  7.7 0.0 copy-start.6
  7.7 0.0 copy-start.5
  7.7 0.0 copy-done.1
  7.7 0.6 %copy-done.6 = s32[1,1,256]{2,1,0:T(1,128)S(1)} copy-done((s32[1,1,256]{2,1,0:T(1,128)S(1)}, s32[1,1,256]{2,1,0:T(1,128)}, u32[]{:S(2)}) %copy-start.6) | copy-done | bytes 1048
  8.4 0.0 copy-done.5
  8.4 0.0 copy-start
  8.4 0.9 %copy-done = f32[2,2,64,256]{3,2,1,0:T(8,128)S(1)} copy-done((f32[2,2,64,256]{3,2,1,0:T(8,128)S(1)}, f32[2,2,64,256]{3,2,1,0:T(8,128)}, u32[]{:S(2)}) %copy-start) | copy-done | bytes 262168
  9.3 0.0 copy-start.3
  9.3 0.9 %copy-done.3 = f32[1,1,256,2,128]{4,3,2,1,0:T(2,128)S(1)} copy-done((f32[1,1,256,2,128]{4,3,2,1,0:T(2,128)S(1)}, f32[1,1,256,2,128]{4,3,2,1,0:T(2,128)}, u32[]{:S(2)}) %copy-start.3) | copy-done | bytes 262168
  10.3 0.0 copy-start.4
  10.3 0.9 %copy-done.4 = f32[1,1,256,128]{3,2,1,0:T(8,128)S(1)} copy-done((f32[1,1,256,128]{3,2,1,0:T(8,128)S(1)}, f32[1,1,256,128]{3,2,1,0:T(8,128)}, u32[]{:S(2)}) %copy-start.4) | copy-done | bytes 131096
  11.2 1.2 %spread_and_inner_rows.1.mixed_ref = f32[8,5,2,8,256]{4,3,2,1,0:T(8,128)S(1)} custom-call(s32[1,256]{1,0:T(1,128)S(1)} %bitcast.14, s32[1,256]{1,0:T(1,128)S(1)} %bitcast.15, f32[512,128]{1,0:T(8,128)S(1)} %bitcast.12, f32[256,128]{1,0:T(8,128)S(1)} %bitcast.13, f32[2,2,64,256]{3,2,1,0:T(8,128)S(1)} %copy-done, f32[2,64,256]{2,1,0:T(8,128)S(1)} %copy-done.1), custom_call_target="tpu_custom_call" | custom-call | flops 1000000000 | bytes 10000000 | tf_op jit(solution)/shard_map/spread_and_inner_rows/pallas_call | solution.py:224
  12.4 0.0 collective-permute-done.1.after_ref
  12.4 0.0 collective-permute-done.before_ref
  12.4 0.8 %end_rows.1 = f32[8,5,2,8,256]{4,3,2,1,0:T(8,128)S(1)} custom-call(f32[2,2,64,256]{3,2,1,0:T(8,128)S(1)} %copy-done, f32[2,64,256]{2,1,0:T(8,128)S(1)} %copy-done.1, f32[3,2,8,256]{3,2,1,0:T(8,128)S(1)} %collective-permute-done.before_ref, f32[3,2,8,256]{3,2,1,0:T(8,128)S(1)} %collective-permute-done.1.after_ref, ...), custom_call_target="tpu_custom_call" | custom-call | flops 10000000 | bytes 1000000 | tf_op jit(solution)/shard_map/end_rows/pallas_call | solution.py:241
  13.2 0.0 copy-start.2
  13.2 15.2 %all_to_all.5.moved_ref = f32[8,5,2,8,256]{4,3,2,1,0:T(8,128)S(1)} all-to-all(f32[8,5,2,8,256]{4,3,2,1,0:T(8,128)S(1)} %end_rows.1), channel_id=1, replica_groups=mesh['sec'=8,'tile'=4] {'sec'}, dimensions={0} | all-to-all | bytes 1310720 | tf_op jit(solution)/shard_map/all_to_all | solution.py:251
  28.5 0.0 copy-done.2
  28.5 1.5 %cross_steps.1 = f32[2,16,8,256]{3,2,1,0:T(8,128)} custom-call(f32[8,5,2,8,256]{4,3,2,1,0:T(8,128)S(1)} %all_to_all.5.moved_ref, f32[16,8,256]{2,1,0:T(8,128)S(1)} %copy-done.2), custom_call_target="tpu_custom_call" | custom-call | flops 10000000 | bytes 800000 | tf_op jit(solution)/shard_map/cross_steps/pallas_call | solution.py:252
Async XLA Ops:
  0.0 7.7 %copy-start.1 = (f32[2,64,256]{2,1,0:T(8,128)S(1)}, f32[2,64,256]{2,1,0:T(8,128)}, u32[]{:S(2)}) copy-start(f32[2,64,256]{2,1,0:T(8,128)} %stiff_ref.4) | copy-start | bytes 393220
  0.8 11.6 %collective-permute-start.1 = (f32[3,2,8,256]{3,2,1,0:T(8,128)S(1)}, f32[3,2,8,256]{3,2,1,0:T(8,128)S(1)}, u32[]{:S(2)}, u32[]{:S(2)}) collective-permute-start(f32[3,2,8,256]{3,2,1,0:T(8,128)S(1)} %get-tuple-element.5), channel_id=1, source_target_pairs={{1,0},{2,1},{3,2},{5,4},{6,5},{7,6},{9,8},{10,9},{11,10},{13,12},{... | collective-permute-start | bytes 147464 | tf_op jit(solution)/shard_map/ppermute | solution.py:222
  2.1 10.3 %collective-permute-start = (f32[3,2,8,256]{3,2,1,0:T(8,128)S(1)}, f32[3,2,8,256]{3,2,1,0:T(8,128)S(1)}, u32[]{:S(2)}, u32[]{:S(2)}) collective-permute-start(f32[3,2,8,256]{3,2,1,0:T(8,128)S(1)} %get-tuple-element.6), channel_id=1, source_target_pairs={{0,1},{1,2},{2,3},{4,5},{5,6},{6,7},{8,9},{9,10},{10,11},{12,13},{... | collective-permute-start | bytes 147464 | tf_op jit(solution)/shard_map/ppermute | solution.py:221
  7.7 0.7 %copy-start.6 = (s32[1,1,256]{2,1,0:T(1,128)S(1)}, s32[1,1,256]{2,1,0:T(1,128)}, u32[]{:S(2)}) copy-start(s32[1,1,256]{2,1,0:T(1,128)} %param.11) | copy-start | bytes 3076
  7.7 0.7 %copy-start.5 = (s32[1,1,256,1]{2,3,1,0:T(1,128)S(1)}, s32[1,1,256,1]{2,3,1,0:T(1,128)}, u32[]{:S(2)}) copy-start(s32[1,1,256,1]{2,3,1,0:T(1,128)} %param.10) | copy-start | bytes 3076
  8.4 0.9 %copy-start = (f32[2,2,64,256]{3,2,1,0:T(8,128)S(1)}, f32[2,2,64,256]{3,2,1,0:T(8,128)}, u32[]{:S(2)}) copy-start(f32[2,2,64,256]{3,2,1,0:T(8,128)} %force_ref.3) | copy-start | bytes 786436
  9.3 0.9 %copy-start.3 = (f32[1,1,256,2,128]{4,3,2,1,0:T(2,128)S(1)}, f32[1,1,256,2,128]{4,3,2,1,0:T(2,128)}, u32[]{:S(2)}) copy-start(f32[1,1,256,2,128]{4,3,2,1,0:T(2,128)} %param.12) | copy-start | bytes 786436
  10.3 0.9 %copy-start.4 = (f32[1,1,256,128]{3,2,1,0:T(8,128)S(1)}, f32[1,1,256,128]{3,2,1,0:T(8,128)}, u32[]{:S(2)}) copy-start(f32[1,1,256,128]{3,2,1,0:T(8,128)} %param.13) | copy-start | bytes 393220
  13.2 15.3 %copy-start.2 = (f32[16,8,256]{2,1,0:T(8,128)S(1)}, f32[16,8,256]{2,1,0:T(8,128)}, u32[]{:S(2)}) copy-start(f32[16,8,256]{2,1,0:T(8,128)} %stiff_ref.5) | copy-start | bytes 393220

commit v4 on v3

--- a/solution.py
+++ b/solution.py
@@ -116,33 +116,27 @@
                     out_ref[o, c, l, :, b * width : (b + 1) * width] = held[c, l, b, at : at + inner_rows, :]
 
 
-def inner_kernel(dest_ref, pos_ref, flow_ref, conf_ref, force_ref, stiff_ref, out_ref, held, *scratch):
-    layers, rows, columns = stiff_ref.shape
+def inner_kernel(dest_ref, pos_ref, flow_ref, conf_ref, own_ref, out_ref, edge_ref, held, *scratch):
+    _, layers, rows, columns = own_ref.shape
     blocks, width = held.shape[2], held.shape[-1]
     spread(layers, out_ref.shape[3], blocks, dest_ref, pos_ref, flow_ref, conf_ref, out_ref)
     for b in range(blocks):
-        span = slice(b * width, (b + 1) * width)
-        for l in range(layers):
-            held[2, l, b] = stiff_ref[l, :, span]
-            for c in range(2):
-                held[c, l, b] = force_ref[c, l, :, span]
+        held[:, :, b] = own_ref[:, :, :, b * width : (b + 1) * width]
+    edge_ref[:, :, :, : 2 * HALO] = held[:, :, :, : 2 * HALO]
+    edge_ref[:, :, :, 2 * HALO :] = held[:, :, :, rows - 2 * HALO :]
     relax(held, *scratch)
     put_rows(held, out_ref, HALO, HALO, rows - HALO)
 
 
-def ends_kernel(force_ref, stiff_ref, before_ref, after_ref, mixed_ref, out_ref, held, *scratch):
-    layers, rows, columns = stiff_ref.shape
+def ends_kernel(edge_ref, before_ref, after_ref, mixed_ref, out_ref, held, *scratch):
     blocks, width = held.shape[2], held.shape[-1]
+    rows = out_ref.shape[0] * out_ref.shape[3]
     edge = HALO // out_ref.shape[3]
+    held[:, :, :, HALO : 5 * HALO] = edge_ref[...]
     for b in range(blocks):
         span = slice(b * width, (b + 1) * width)
-        for c in range(3):
-            for l in range(layers):
-                own = stiff_ref.at[l] if c == 2 else force_ref.at[c, l]
-                held[c, l, b, :HALO] = before_ref[c, l, :, span]
-                held[c, l, b, HALO : 3 * HALO] = own[: 2 * HALO, span]
-                held[c, l, b, 3 * HALO : 5 * HALO] = own[rows - 2 * HALO :, span]
-                held[c, l, b, 5 * HALO :] = after_ref[c, l, :, span]
+        held[:, :, b, :HALO] = before_ref[:, :, :, span]
+        held[:, :, b, 5 * HALO :] = after_ref[:, :, :, span]
     out_ref[:, 2:] = mixed_ref[:, 2:]
     out_ref[edge:-edge, :2] = mixed_ref[edge:-edge, :2]
     relax(held, *scratch)
@@ -213,19 +207,17 @@
     up = [(i, i + 1) for i in range(tiles - 1)]
     down = [(j, i) for i, j in up]
 
-    def ends(field):
-        cut = field.reshape(field.shape[0], layers, rows // HALO, HALO, columns)
-        return cut[:, :, :: rows // HALO - 1]
-
-    edges = jnp.pad(ends(in_plane_force), ((0, 1),) + ((0, 0),) * 4) + jnp.pad(ends(stiffness[None]), ((2, 0),) + ((0, 0),) * 4)
-    before = lax.ppermute(edges[:, :, 1], "tile", up)
-    after = lax.ppermute(edges[:, :, 0], "tile", down)
+    rest = ((0, 0),) * 3
+    own = jnp.pad(in_plane_force, ((0, 1),) + rest) + jnp.pad(stiffness[None], ((2, 0),) + rest)
+
+    before = lax.ppermute(own[:, :, rows - HALO :], "tile", up)
+    after = lax.ppermute(own[:, :, :HALO], "tile", down)
     mixed_shape = jax.ShapeDtypeStruct((groups, 5, layers, inner_rows, columns), jnp.float32)
-    mixed = pl.pallas_call(
+    mixed, own_edges = pl.pallas_call(
         inner_kernel,
-        out_shape=mixed_shape,
-        in_specs=[VMEM] * 6,
-        out_specs=VMEM,
+        out_shape=[mixed_shape, jax.ShapeDtypeStruct((3, layers, blocks, 4 * HALO, width), jnp.float32)],
+        in_specs=[VMEM] * 5,
+        out_specs=[VMEM] * 2,
         scratch_shapes=relax_scratch(layers, blocks, rows, width),
         compiler_params=LIMIT,
         cost_estimate=pl.CostEstimate(flops=10**9, bytes_accessed=10**7, transcendentals=0),
@@ -235,19 +227,18 @@
         patch_pos.reshape(1, count),
         patch_flow.reshape(count * 2, width),
         patch_conf.reshape(count, width),
-        in_plane_force,
-        stiffness,
+        own,
     )
     mixed = pl.pallas_call(
         ends_kernel,
         out_shape=mixed_shape,
-        in_specs=[VMEM] * 5,
+        in_specs=[VMEM] * 4,
         out_specs=VMEM,
         scratch_shapes=relax_scratch(layers, blocks, 6 * HALO, width),
         compiler_params=LIMIT,
         cost_estimate=pl.CostEstimate(flops=10**7, bytes_accessed=10**6, transcendentals=0),
         name="end_rows",
-    )(in_plane_force, stiffness, before, after, mixed)
+    )(own_edges, before, after, mixed)
     moved = lax.all_to_all(mixed, "sec", split_axis=0, concat_axis=0, tiled=True)
     return pl.pallas_call(
         cross_kernel,

time: 30.3 us -> 27.6 us (0.911)
  local copies, waits for them, and re-layouts: 3.48 us -> 0.68 us
    unnamed x14, local copies, waits for them, and re-layouts: 3.48 us -> 0.68 us
    add x0 -> x2, other arithmetic: none -> 0.87 us  [per_device(): jnp.pad(in_plane_force, ((0, 1),) + rest)]
    squeeze x1 -> x0, other arithmetic: 0.82 us -> none  [per_device(): after = lax.ppermute(edges[:, :, 0], 'tile', down)]
where the time goes in v4:
time: 27.6 us; the launch traced here: 27.4 us
  blocking collectives  15.2 us (55%)
  starting transfers between devices  6.98 us (25%)
  Pallas kernels  3.49 us (13%)
  other arithmetic  0.87 us (3%)
  local copies, waits for them, and re-layouts  0.68 us (2%)
    all_to_all x1, blocking collectives, per_device(): lax.all_to_all(mixed, 'sec', split_axis=0, concat_axis=0, tiled=True)  15.2 us
    ppermute x1, starting transfers between devices, per_device(): before = lax.ppermute(own[:, :, rows - HALO:], 'tile', up)  5.69 us
    pallas_call x1, Pallas kernels, per_device(): pl.pallas_call(cross_kernel, out_shape=jax.ShapeDtypeStruct((2, groups *...  1.49 us
    ppermute x1, starting transfers between devices, per_device(): after = lax.ppermute(own[:, :, :HALO], 'tile', down)  1.29 us
    pallas_call x1, Pallas kernels, per_device(): pl.pallas_call(inner_kernel, out_shape=[mixed_shape, jax.ShapeDtypeStruct...  1.18 us
    add x2, other arithmetic, per_device(): jnp.pad(in_plane_force, ((0, 1),) + rest)  0.87 us
    pallas_call x1, Pallas kernels, per_device(): pl.pallas_call(ends_kernel, out_shape=mixed_shape, in_specs=[VMEM] * 4, o...  0.82 us
    unnamed x14, local copies, waits for them, and re-layouts  0.68 us
  transfers between devices with their start and end apart: 2, of which 0 were waited for; matrix products, arithmetic and copies ran while one was open for 0% of the time, Pallas kernels for 4%

profile of v4, /device:TPU:0, one launch (start us, length us, event | category | flops | bytes accessed | tf_op | source)
XLA Modules:
  0.0 27.4 jit_solution(10089722898244415184)
XLA Ops:
  0.0 0.0 copy-start.5
  0.0 0.0 copy-start.6
  0.0 0.8 %fusion.1 = (f32[3,2,8,256]{3,2,1,0:T(8,128)S(1)}, f32[3,2,8,256]{3,2,1,0:T(8,128)S(1)}) fusion(f32[2,2,64,256]{3,2,1,0:T(8,128)} %param.7, f32[1,2,64,256]{3,2,1,0:T(8,128)} %bitcast.9), kind=kLoop, calls=%fused_computation.6 | loop fusion | flops 24576 | bytes 491520 | tf_op jit(solution)/shard_map/add | solution.py:211
  0.8 1.3 %collective-permute-start.1 = (f32[3,2,8,256]{3,2,1,0:T(8,128)S(1)}, f32[3,2,8,256]{3,2,1,0:T(8,128)S(1)}, u32[]{:S(2)}, u32[]{:S(2)}) collective-permute-start(f32[3,2,8,256]{3,2,1,0:T(8,128)S(1)} %get-tuple-element.9), channel_id=1, source_target_pairs={{1,0},{2,1},{3,2},{5,4},{6,5},{7,6},{9,8},{10,9},{11,10},{13,12},{... | collective-permute-start | bytes 147464 | tf_op jit(solution)/shard_map/ppermute | solution.py:214
  2.1 0.0 copy-start.1
  2.2 0.0 copy-start.2
  2.2 5.7 %collective-permute-start = (f32[3,2,8,256]{3,2,1,0:T(8,128)S(1)}, f32[3,2,8,256]{3,2,1,0:T(8,128)S(1)}, u32[]{:S(2)}, u32[]{:S(2)}) collective-permute-start(f32[3,2,8,256]{3,2,1,0:T(8,128)S(1)} %get-tuple-element.10), channel_id=1, source_target_pairs={{0,1},{1,2},{2,3},{4,5},{5,6},{6,7},{8,9},{9,10},{10,11},{12,13},{... | collective-permute-start | bytes 147464 | tf_op jit(solution)/shard_map/ppermute | solution.py:213
  7.9 0.0 copy-done.5
  7.9 0.0 copy-done.6
  7.9 0.0 copy-start.4
  7.9 0.0 copy-start.3
  7.9 0.0 copy-done.1
  8.0 0.0 copy-done.2
  8.0 0.6 %copy-done.4 = s32[1,1,256]{2,1,0:T(1,128)S(1)} copy-done((s32[1,1,256]{2,1,0:T(1,128)S(1)}, s32[1,1,256]{2,1,0:T(1,128)}, u32[]{:S(2)}) %copy-start.4) | copy-done | bytes 1048
  8.6 0.0 copy-done.3
  8.6 1.2 %spread_and_inner_rows.1 = (f32[8,5,2,8,256]{4,3,2,1,0:T(8,128)S(1)}, f32[3,2,2,32,128]{4,3,2,1,0:T(8,128)S(1)}) custom-call(s32[1,256]{1,0:T(1,128)S(1)} %bitcast.7, s32[1,256]{1,0:T(1,128)S(1)} %bitcast.8, f32[512,128]{1,0:T(8,128)S(1)} %bitcast.5, f32[256,128]{1,0:T(8,128)S(1)} %bitcast.6, f32[3,2,64,256]{3,2,1,0:T(8,128)S(1)} %pad_add_fusion.own_ref), custom_call_target="tpu_custom_call" | custom-call | flops 1000000000 | bytes 10000000 | tf_op jit(solution)/shard_map/spread_and_inner_rows/pallas_call | solution.py:216
  9.8 0.0 collective-permute-done.1.after_ref
  9.8 0.0 collective-permute-done.before_ref
  9.8 0.8 %end_rows.1 = f32[8,5,2,8,256]{4,3,2,1,0:T(8,128)S(1)} custom-call(f32[3,2,2,32,128]{4,3,2,1,0:T(8,128)S(1)} %get-tuple-element.7.edge_ref, f32[3,2,8,256]{3,2,1,0:T(8,128)S(1)} %collective-permute-done.before_ref, f32[3,2,8,256]{3,2,1,0:T(8,128)S(1)} %collective-permute-done.1.after_ref, f32[8,5,2,8,256]{4,3,2,1,0:T(8,128)S(1)} %get-tuple-element.8.mixed_ref), custom_call_target="tpu_custom_call" | custom-call | flops 10000000 | bytes 1000000 | tf_op jit(solution)/shard_map/end_rows/pallas_call | solution.py:232
  10.6 0.0 copy-start
  10.7 15.2 %all_to_all.5.moved_ref = f32[8,5,2,8,256]{4,3,2,1,0:T(8,128)S(1)} all-to-all(f32[8,5,2,8,256]{4,3,2,1,0:T(8,128)S(1)} %end_rows.1), channel_id=1, replica_groups=mesh['sec'=8,'tile'=4] {'sec'}, dimensions={0} | all-to-all | bytes 1310720 | tf_op jit(solution)/shard_map/all_to_all | solution.py:242
  25.9 0.0 copy-done
  25.9 1.5 %cross_steps.1 = f32[2,16,8,256]{3,2,1,0:T(8,128)} custom-call(f32[8,5,2,8,256]{4,3,2,1,0:T(8,128)S(1)} %all_to_all.5.moved_ref, f32[16,8,256]{2,1,0:T(8,128)S(1)} %copy-done), custom_call_target="tpu_custom_call" | custom-call | flops 10000000 | bytes 800000 | tf_op jit(solution)/shard_map/cross_steps/pallas_call | solution.py:243
  (1 shorter events, 0.0 us)
Async XLA Ops:
  0.0 7.9 %copy-start.5 = (f32[2,2,64,256]{3,2,1,0:T(8,128)S(1)}, f32[2,2,64,256]{3,2,1,0:T(8,128)}, u32[]{:S(2)}) copy-start(f32[2,2,64,256]{3,2,1,0:T(8,128)} %param.7) | copy-start | bytes 786436
  0.0 7.9 %copy-start.6 = (f32[2,64,256]{2,1,0:T(8,128)S(1)}, f32[2,64,256]{2,1,0:T(8,128)}, u32[]{:S(2)}) copy-start(f32[2,64,256]{2,1,0:T(8,128)} %param.8) | copy-start | bytes 393220
  0.8 9.0 %collective-permute-start.1 = (f32[3,2,8,256]{3,2,1,0:T(8,128)S(1)}, f32[3,2,8,256]{3,2,1,0:T(8,128)S(1)}, u32[]{:S(2)}, u32[]{:S(2)}) collective-permute-start(f32[3,2,8,256]{3,2,1,0:T(8,128)S(1)} %get-tuple-element.9), channel_id=1, source_target_pairs={{1,0},{2,1},{3,2},{5,4},{6,5},{7,6},{9,8},{10,9},{11,10},{13,12},{... | collective-permute-start | bytes 147464 | tf_op jit(solution)/shard_map/ppermute | solution.py:214
  2.1 5.8 %copy-start.1 = (f32[1,1,256,2,128]{4,3,2,1,0:T(2,128)S(1)}, f32[1,1,256,2,128]{4,3,2,1,0:T(2,128)}, u32[]{:S(2)}) copy-start(f32[1,1,256,2,128]{4,3,2,1,0:T(2,128)} %param.12) | copy-start | bytes 786436
  2.2 5.8 %copy-start.2 = (f32[1,1,256,128]{3,2,1,0:T(8,128)S(1)}, f32[1,1,256,128]{3,2,1,0:T(8,128)}, u32[]{:S(2)}) copy-start(f32[1,1,256,128]{3,2,1,0:T(8,128)} %param.13) | copy-start | bytes 393220
  2.2 7.6 %collective-permute-start = (f32[3,2,8,256]{3,2,1,0:T(8,128)S(1)}, f32[3,2,8,256]{3,2,1,0:T(8,128)S(1)}, u32[]{:S(2)}, u32[]{:S(2)}) collective-permute-start(f32[3,2,8,256]{3,2,1,0:T(8,128)S(1)} %get-tuple-element.10), channel_id=1, source_target_pairs={{0,1},{1,2},{2,3},{4,5},{5,6},{6,7},{8,9},{9,10},{10,11},{12,13},{... | collective-permute-start | bytes 147464 | tf_op jit(solution)/shard_map/ppermute | solution.py:213
  7.9 0.7 %copy-start.4 = (s32[1,1,256]{2,1,0:T(1,128)S(1)}, s32[1,1,256]{2,1,0:T(1,128)}, u32[]{:S(2)}) copy-start(s32[1,1,256]{2,1,0:T(1,128)} %param.11) | copy-start | bytes 3076
  7.9 0.7 %copy-start.3 = (s32[1,1,256,1]{2,3,1,0:T(1,128)S(1)}, s32[1,1,256,1]{2,3,1,0:T(1,128)}, u32[]{:S(2)}) copy-start(s32[1,1,256,1]{2,3,1,0:T(1,128)} %param.10) | copy-start | bytes 3076
  10.6 15.3 %copy-start = (f32[16,8,256]{2,1,0:T(8,128)S(1)}, f32[16,8,256]{2,1,0:T(8,128)}, u32[]{:S(2)}) copy-start(f32[16,8,256]{2,1,0:T(8,128)} %stiff_ref.1) | copy-start | bytes 393220

commit v5 on v4

--- a/solution.py
+++ b/solution.py
@@ -128,15 +128,17 @@
     put_rows(held, out_ref, HALO, HALO, rows - HALO)
 
 
-def ends_kernel(edge_ref, before_ref, after_ref, mixed_ref, out_ref, held, *scratch):
+def ends_kernel(odd_ref, edge_ref, two_ref, one_ref, mixed_ref, out_ref, held, *scratch):
     blocks, width = held.shape[2], held.shape[-1]
     rows = out_ref.shape[0] * out_ref.shape[3]
     edge = HALO // out_ref.shape[3]
     held[:, :, :, HALO : 5 * HALO] = edge_ref[...]
+    odd = odd_ref[0] == 1
     for b in range(blocks):
         span = slice(b * width, (b + 1) * width)
-        held[:, :, b, :HALO] = before_ref[:, :, :, span]
-        held[:, :, b, 5 * HALO :] = after_ref[:, :, :, span]
+        one, two = one_ref[:, :, :, span], two_ref[:, :, :, span]
+        held[:, :, b, :HALO] = jnp.where(odd, one, two)
+        held[:, :, b, 5 * HALO :] = jnp.where(odd, two, one)
     out_ref[:, 2:] = mixed_ref[:, 2:]
     out_ref[edge:-edge, :2] = mixed_ref[edge:-edge, :2]
     relax(held, *scratch)
@@ -204,14 +206,15 @@
     width = patch_flow.shape[-1]
     blocks = columns // width
     count = patch_pos.shape[2]
-    up = [(i, i + 1) for i in range(tiles - 1)]
-    down = [(j, i) for i, j in up]
+    swaps = [[pair for i in range(n, tiles - 1, 2) for pair in ((i, i + 1), (i + 1, i))] for n in range(2)]
+    odd = lax.axis_index("tile") & 1
 
     rest = ((0, 0),) * 3
     own = jnp.pad(in_plane_force, ((0, 1),) + rest) + jnp.pad(stiffness[None], ((2, 0),) + rest)
 
-    before = lax.ppermute(own[:, :, rows - HALO :], "tile", up)
-    after = lax.ppermute(own[:, :, :HALO], "tile", down)
+    first, last = own[:, :, :HALO], own[:, :, rows - HALO :]
+    two = lax.ppermute(jnp.where(odd == 1, last, first), "tile", swaps[1])
+    one = lax.ppermute(jnp.where(odd == 1, first, last), "tile", swaps[0])
     mixed_shape = jax.ShapeDtypeStruct((groups, 5, layers, inner_rows, columns), jnp.float32)
     mixed, own_edges = pl.pallas_call(
         inner_kernel,
@@ -232,13 +235,13 @@
     mixed = pl.pallas_call(
         ends_kernel,
         out_shape=mixed_shape,
-        in_specs=[VMEM] * 4,
+        in_specs=[pl.BlockSpec(memory_space=pltpu.SMEM)] + [VMEM] * 4,
         out_specs=VMEM,
         scratch_shapes=relax_scratch(layers, blocks, 6 * HALO, width),
         compiler_params=LIMIT,
         cost_estimate=pl.CostEstimate(flops=10**7, bytes_accessed=10**6, transcendentals=0),
         name="end_rows",
-    )(own_edges, before, after, mixed)
+    )(odd.reshape(1), own_edges, two, one, mixed)
     moved = lax.all_to_all(mixed, "sec", split_axis=0, concat_axis=0, tiled=True)
     return pl.pallas_call(
         cross_kernel,

time: 27.6 us -> 26 us (0.942)
  the two profiles are of different devices: /device:TPU:0 before, /device:TPU:16 now
where the time goes in v5:
time: 26 us; the launch traced here: 25.8 us
  blocking collectives  14.8 us (57%)
  starting transfers between devices  3.68 us (14%)
  Pallas kernels  3.5 us (13%)
  waiting for transfers between devices  2.11 us (8%)
  other arithmetic  0.97 us (4%)
  local copies, waits for them, and re-layouts  0.68 us (3%)
    all_to_all x1, blocking collectives, per_device(): lax.all_to_all(mixed, 'sec', split_axis=0, concat_axis=0, tiled=True)  14.8 us
    ppermute x1, waiting for transfers between devices, per_device(): two = lax.ppermute(jnp.where(odd == 1, last, first), 'tile', swaps[1])  2.11 us
    ppermute x1, starting transfers between devices, per_device(): two = lax.ppermute(jnp.where(odd == 1, last, first), 'tile', swaps[1])  2.04 us
    ppermute x1, starting transfers between devices, per_device(): one = lax.ppermute(jnp.where(odd == 1, first, last), 'tile', swaps[0])  1.64 us
    pallas_call x1, Pallas kernels, per_device(): pl.pallas_call(cross_kernel, out_shape=jax.ShapeDtypeStruct((2, groups *...  1.49 us
    pallas_call x1, Pallas kernels, per_device(): pl.pallas_call(inner_kernel, out_shape=[mixed_shape, jax.ShapeDtypeStruct...  1.18 us
    select_n x1, other arithmetic, per_device(): one = lax.ppermute(jnp.where(odd == 1, first, last), 'tile', swaps[0])  0.94 us
    pallas_call x1, Pallas kernels, per_device(): pl.pallas_call(ends_kernel, out_shape=mixed_shape, in_specs=[pl.BlockSpec...  0.82 us
  transfers between devices with their start and end apart: 2, of which 1 were waited for; matrix products, arithmetic and copies ran while one was open for 0% of the time, Pallas kernels for 5%

profile of v5, /device:TPU:16, one launch (start us, length us, event | category | flops | bytes accessed | tf_op | source)
XLA Modules:
  0.0 25.8 jit_solution(17760256824531144032)
XLA Ops:
  0.0 0.0 copy-start.5
  0.0 0.0 copy-start.6
  0.0 0.9 %broadcast_select_fusion = (f32[3,2,8,256]{3,2,1,0:T(8,128)S(1)}, f32[3,2,8,256]{3,2,1,0:T(8,128)S(1)}) fusion(pred[]{:T(512)S(6)} %eq.4, f32[1,2,64,256]{3,2,1,0:T(8,128)} %bitcast.10, f32[2,2,64,256]{3,2,1,0:T(8,128)} %param.7), kind=kLoop, calls=%fused_computation.7 | loop fusion | flops 73728 | bytes 491521 | tf_op jit(solution)/shard_map/jit(_where)/select_n | solution.py:217
  0.9 1.6 %collective-permute-start.1 = (f32[3,2,8,256]{3,2,1,0:T(8,128)S(1)}, f32[3,2,8,256]{3,2,1,0:T(8,128)S(1)}, u32[]{:S(2)}, u32[]{:S(2)}) collective-permute-start(f32[3,2,8,256]{3,2,1,0:T(8,128)S(1)} %get-tuple-element.9), channel_id=1, source_target_pairs={{0,1},{1,0},{2,3},{3,2},{4,5},{5,4},{6,7},{7,6},{8,9},{9,8},{10,11... | collective-permute-start | bytes 147464 | tf_op jit(solution)/shard_map/ppermute | solution.py:217
  2.6 0.0 copy-start.1
  2.6 0.0 copy-start.2
  2.6 2.0 %collective-permute-start = (f32[3,2,8,256]{3,2,1,0:T(8,128)S(1)}, f32[3,2,8,256]{3,2,1,0:T(8,128)S(1)}, u32[]{:S(2)}, u32[]{:S(2)}) collective-permute-start(f32[3,2,8,256]{3,2,1,0:T(8,128)S(1)} %get-tuple-element.10), channel_id=1, source_target_pairs={{1,2},{2,1},{5,6},{6,5},{9,10},{10,9},{13,14},{14,13},{17,18},{18,... | collective-permute-start | bytes 147464 | tf_op jit(solution)/shard_map/ppermute | solution.py:216
  4.6 0.0 copy-done.5
  4.6 0.0 copy-done.6
  4.7 0.0 copy-start.4
  4.7 0.0 copy-start.3
  4.7 0.0 copy-done.1
  4.7 0.0 copy-done.2
  4.7 0.6 %copy-done.4 = s32[1,1,256]{2,1,0:T(1,128)S(1)} copy-done((s32[1,1,256]{2,1,0:T(1,128)S(1)}, s32[1,1,256]{2,1,0:T(1,128)}, u32[]{:S(2)}) %copy-start.4) | copy-done | bytes 1048
  5.3 0.0 copy-done.3
  5.4 1.2 %spread_and_inner_rows.1 = (f32[8,5,2,8,256]{4,3,2,1,0:T(8,128)S(1)}, f32[3,2,2,32,128]{4,3,2,1,0:T(8,128)S(1)}) custom-call(s32[1,256]{1,0:T(1,128)S(1)} %bitcast.8, s32[1,256]{1,0:T(1,128)S(1)} %bitcast.9, f32[512,128]{1,0:T(8,128)S(1)} %bitcast.6, f32[256,128]{1,0:T(8,128)S(1)} %bitcast.7, f32[3,2,64,256]{3,2,1,0:T(8,128)S(1)} %pad_add_fusion.own_ref), custom_call_target="tpu_custom_call" | custom-call | flops 1000000000 | bytes 10000000 | tf_op jit(solution)/shard_map/spread_and_inner_rows/pallas_call | solution.py:219
  6.6 0.0 collective-permute-done.1.one_ref
  6.6 2.1 %collective-permute-done.two_ref = f32[3,2,8,256]{3,2,1,0:T(8,128)S(1)} collective-permute-done((f32[3,2,8,256]{3,2,1,0:T(8,128)S(1)}, f32[3,2,8,256]{3,2,1,0:T(8,128)S(1)}, u32[]{:S(2)}, u32[]{:S(2)}) %collective-permute-start) | collective-permute-done | bytes 49184 | tf_op jit(solution)/shard_map/ppermute | solution.py:216
  8.7 0.8 %end_rows.1 = f32[8,5,2,8,256]{4,3,2,1,0:T(8,128)S(1)} custom-call(s32[1]{0:T(128)} %bitcast.odd_ref, f32[3,2,2,32,128]{4,3,2,1,0:T(8,128)S(1)} %get-tuple-element.7.edge_ref, f32[3,2,8,256]{3,2,1,0:T(8,128)S(1)} %collective-permute-done.two_ref, f32[3,2,8,256]{3,2,1,0:T(8,128)S(1)} %collective-permute-done.1.one_ref, ...), custom_call_target="tpu_custom_call" | custom-call | flops 10000000 | bytes 1000000 | tf_op jit(solution)/shard_map/end_rows/pallas_call | solution.py:235
  9.5 0.0 copy-start
  9.5 14.8 %all_to_all.5.moved_ref = f32[8,5,2,8,256]{4,3,2,1,0:T(8,128)S(1)} all-to-all(f32[8,5,2,8,256]{4,3,2,1,0:T(8,128)S(1)} %end_rows.1), channel_id=1, replica_groups=mesh['sec'=8,'tile'=4] {'sec'}, dimensions={0} | all-to-all | bytes 1310720 | tf_op jit(solution)/shard_map/all_to_all | solution.py:245
  24.3 0.0 copy-done
  24.3 1.5 %cross_steps.1 = f32[2,16,8,256]{3,2,1,0:T(8,128)} custom-call(f32[8,5,2,8,256]{4,3,2,1,0:T(8,128)S(1)} %all_to_all.5.moved_ref, f32[16,8,256]{2,1,0:T(8,128)S(1)} %copy-done), custom_call_target="tpu_custom_call" | custom-call | flops 10000000 | bytes 800000 | tf_op jit(solution)/shard_map/cross_steps/pallas_call | solution.py:246
  (1 shorter events, 0.0 us)
Async XLA Ops:
  0.0 4.6 %copy-start.5 = (f32[2,2,64,256]{3,2,1,0:T(8,128)S(1)}, f32[2,2,64,256]{3,2,1,0:T(8,128)}, u32[]{:S(2)}) copy-start(f32[2,2,64,256]{3,2,1,0:T(8,128)} %param.7) | copy-start | bytes 786436
  0.0 4.6 %copy-start.6 = (f32[2,64,256]{2,1,0:T(8,128)S(1)}, f32[2,64,256]{2,1,0:T(8,128)}, u32[]{:S(2)}) copy-start(f32[2,64,256]{2,1,0:T(8,128)} %param.8) | copy-start | bytes 393220
  0.9 5.6 %collective-permute-start.1 = (f32[3,2,8,256]{3,2,1,0:T(8,128)S(1)}, f32[3,2,8,256]{3,2,1,0:T(8,128)S(1)}, u32[]{:S(2)}, u32[]{:S(2)}) collective-permute-start(f32[3,2,8,256]{3,2,1,0:T(8,128)S(1)} %get-tuple-element.9), channel_id=1, source_target_pairs={{0,1},{1,0},{2,3},{3,2},{4,5},{5,4},{6,7},{7,6},{8,9},{9,8},{10,11... | collective-permute-start | bytes 147464 | tf_op jit(solution)/shard_map/ppermute | solution.py:217
  2.6 2.1 %copy-start.1 = (f32[1,1,256,2,128]{4,3,2,1,0:T(2,128)S(1)}, f32[1,1,256,2,128]{4,3,2,1,0:T(2,128)}, u32[]{:S(2)}) copy-start(f32[1,1,256,2,128]{4,3,2,1,0:T(2,128)} %param.12) | copy-start | bytes 786436
  2.6 2.1 %copy-start.2 = (f32[1,1,256,128]{3,2,1,0:T(8,128)S(1)}, f32[1,1,256,128]{3,2,1,0:T(8,128)}, u32[]{:S(2)}) copy-start(f32[1,1,256,128]{3,2,1,0:T(8,128)} %param.13) | copy-start | bytes 393220
  2.6 6.1 %collective-permute-start = (f32[3,2,8,256]{3,2,1,0:T(8,128)S(1)}, f32[3,2,8,256]{3,2,1,0:T(8,128)S(1)}, u32[]{:S(2)}, u32[]{:S(2)}) collective-permute-start(f32[3,2,8,256]{3,2,1,0:T(8,128)S(1)} %get-tuple-element.10), channel_id=1, source_target_pairs={{1,2},{2,1},{5,6},{6,5},{9,10},{10,9},{13,14},{14,13},{17,18},{18,... | collective-permute-start | bytes 147464 | tf_op jit(solution)/shard_map/ppermute | solution.py:216
  4.7 0.7 %copy-start.4 = (s32[1,1,256]{2,1,0:T(1,128)S(1)}, s32[1,1,256]{2,1,0:T(1,128)}, u32[]{:S(2)}) copy-start(s32[1,1,256]{2,1,0:T(1,128)} %param.11) | copy-start | bytes 3076
  4.7 0.7 %copy-start.3 = (s32[1,1,256,1]{2,3,1,0:T(1,128)S(1)}, s32[1,1,256,1]{2,3,1,0:T(1,128)}, u32[]{:S(2)}) copy-start(s32[1,1,256,1]{2,3,1,0:T(1,128)} %param.10) | copy-start | bytes 3076
  9.5 14.8 %copy-start = (f32[16,8,256]{2,1,0:T(8,128)S(1)}, f32[16,8,256]{2,1,0:T(8,128)}, u32[]{:S(2)}) copy-start(f32[16,8,256]{2,1,0:T(8,128)} %stiff_ref.1) | copy-start | bytes 393220

commit v6 on v5

--- a/solution.py
+++ b/solution.py
@@ -1,3 +1,5 @@
+import functools
+
 import jax
 import jax.numpy as jnp
 from jax import lax
@@ -128,17 +130,18 @@
     put_rows(held, out_ref, HALO, HALO, rows - HALO)
 
 
-def ends_kernel(odd_ref, edge_ref, two_ref, one_ref, mixed_ref, out_ref, held, *scratch):
+def ends_kernel(tiles, tile_ref, edge_ref, two_ref, one_ref, mixed_ref, out_ref, held, *scratch):
     blocks, width = held.shape[2], held.shape[-1]
     rows = out_ref.shape[0] * out_ref.shape[3]
     edge = HALO // out_ref.shape[3]
     held[:, :, :, HALO : 5 * HALO] = edge_ref[...]
-    odd = odd_ref[0] == 1
+    tile = tile_ref[0]
+    odd = (tile & 1) == 1
     for b in range(blocks):
         span = slice(b * width, (b + 1) * width)
         one, two = one_ref[:, :, :, span], two_ref[:, :, :, span]
-        held[:, :, b, :HALO] = jnp.where(odd, one, two)
-        held[:, :, b, 5 * HALO :] = jnp.where(odd, two, one)
+        held[:, :, b, :HALO] = jnp.where(tile == 0, 0.0, jnp.where(odd, one, two))
+        held[:, :, b, 5 * HALO :] = jnp.where(tile == tiles - 1, 0.0, jnp.where(odd, two, one))
     out_ref[:, 2:] = mixed_ref[:, 2:]
     out_ref[edge:-edge, :2] = mixed_ref[edge:-edge, :2]
     relax(held, *scratch)
@@ -206,8 +209,12 @@
     width = patch_flow.shape[-1]
     blocks = columns // width
     count = patch_pos.shape[2]
-    swaps = [[pair for i in range(n, tiles - 1, 2) for pair in ((i, i + 1), (i + 1, i))] for n in range(2)]
-    odd = lax.axis_index("tile") & 1
+    swaps = []
+    for n in range(2):
+        other = [i + 1 if i % 2 == n else i - 1 for i in range(tiles)]
+        swaps.append([(i, j if 0 <= j < tiles else i) for i, j in enumerate(other)])
+    tile = lax.axis_index("tile")
+    odd = tile & 1
 
     rest = ((0, 0),) * 3
     own = jnp.pad(in_plane_force, ((0, 1),) + rest) + jnp.pad(stiffness[None], ((2, 0),) + rest)
@@ -233,7 +240,7 @@
         own,
     )
     mixed = pl.pallas_call(
-        ends_kernel,
+        functools.partial(ends_kernel, tiles),
         out_shape=mixed_shape,
         in_specs=[pl.BlockSpec(memory_space=pltpu.SMEM)] + [VMEM] * 4,
         out_specs=VMEM,
@@ -241,7 +248,7 @@
         compiler_params=LIMIT,
         cost_estimate=pl.CostEstimate(flops=10**7, bytes_accessed=10**6, transcendentals=0),
         name="end_rows",
-    )(odd.reshape(1), own_edges, two, one, mixed)
+    )(tile.reshape(1), own_edges, two, one, mixed)
     moved = lax.all_to_all(mixed, "sec", split_axis=0, concat_axis=0, tiled=True)
     return pl.pallas_call(
         cross_kernel,

time: 26 us -> 26 us (level)
  no operation moved by 1% of the time
where the time goes in v6:
time: 26 us; the launch traced here: 25.8 us
  blocking collectives  14.8 us (57%)
  starting transfers between devices  3.68 us (14%)
  Pallas kernels  3.5 us (13%)
  waiting for transfers between devices  2.11 us (8%)
  other arithmetic  0.97 us (4%)
  local copies, waits for them, and re-layouts  0.68 us (3%)
    all_to_all x1, blocking collectives, per_device(): lax.all_to_all(mixed, 'sec', split_axis=0, concat_axis=0, tiled=True)  14.8 us
    ppermute x1, waiting for transfers between devices, per_device(): two = lax.ppermute(jnp.where(odd == 1, last, first), 'tile', swaps[1])  2.11 us
    ppermute x1, starting transfers between devices, per_device(): two = lax.ppermute(jnp.where(odd == 1, last, first), 'tile', swaps[1])  2.04 us
    ppermute x1, starting transfers between devices, per_device(): one = lax.ppermute(jnp.where(odd == 1, first, last), 'tile', swaps[0])  1.64 us
    pallas_call x1, Pallas kernels, per_device(): pl.pallas_call(cross_kernel, out_shape=jax.ShapeDtypeStruct((2, groups *...  1.49 us
    pallas_call x1, Pallas kernels, per_device(): pl.pallas_call(inner_kernel, out_shape=[mixed_shape, jax.ShapeDtypeStruct...  1.18 us
    select_n x1, other arithmetic, per_device(): one = lax.ppermute(jnp.where(odd == 1, first, last), 'tile', swaps[0])  0.94 us
    pallas_call x1, Pallas kernels, per_device(): pl.pallas_call(functools.partial(ends_kernel, tiles), out_shape=mixed_sha...  0.82 us
  transfers between devices with their start and end apart: 2, of which 1 were waited for; matrix products, arithmetic and copies ran while one was open for 0% of the time, Pallas kernels for 5%

profile of v6, /device:TPU:16, one launch (start us, length us, event | category | flops | bytes accessed | tf_op | source)
XLA Modules:
  0.0 25.8 jit_solution(6689937846476927936)
XLA Ops:
  0.0 0.0 copy-start.5
  0.0 0.0 copy-start.6
  0.0 0.9 %broadcast_select_fusion = (f32[3,2,8,256]{3,2,1,0:T(8,128)S(1)}, f32[3,2,8,256]{3,2,1,0:T(8,128)S(1)}) fusion(pred[]{:T(512)S(6)} %eq.4, f32[1,2,64,256]{3,2,1,0:T(8,128)} %bitcast.10, f32[2,2,64,256]{3,2,1,0:T(8,128)} %param.7), kind=kLoop, calls=%fused_computation.7 | loop fusion | flops 73728 | bytes 491521 | tf_op jit(solution)/shard_map/jit(_where)/select_n | solution.py:224
  0.9 1.6 %collective-permute-start.1 = (f32[3,2,8,256]{3,2,1,0:T(8,128)S(1)}, f32[3,2,8,256]{3,2,1,0:T(8,128)S(1)}, u32[]{:S(2)}, u32[]{:S(2)}) collective-permute-start(f32[3,2,8,256]{3,2,1,0:T(8,128)S(1)} %get-tuple-element.9), channel_id=1, source_target_pairs={{0,1},{1,0},{2,3},{3,2},{4,5},{5,4},{6,7},{7,6},{8,9},{9,8},{10,11... | collective-permute-start | bytes 147464 | tf_op jit(solution)/shard_map/ppermute | solution.py:224
  2.6 0.0 copy-start.1
  2.6 0.0 copy-start.2
  2.6 2.0 %collective-permute-start = (f32[3,2,8,256]{3,2,1,0:T(8,128)S(1)}, f32[3,2,8,256]{3,2,1,0:T(8,128)S(1)}, u32[]{:S(2)}, u32[]{:S(2)}) collective-permute-start(f32[3,2,8,256]{3,2,1,0:T(8,128)S(1)} %get-tuple-element.10), channel_id=1, source_target_pairs={{0,0},{1,2},{2,1},{3,3},{4,4},{5,6},{6,5},{7,7},{8,8},{9,10},{10,9... | collective-permute-start | bytes 147464 | tf_op jit(solution)/shard_map/ppermute | solution.py:223
  4.6 0.0 copy-done.5
  4.6 0.0 copy-done.6
  4.7 0.0 copy-start.4
  4.7 0.0 copy-start.3
  4.7 0.0 copy-done.1
  4.7 0.0 copy-done.2
  4.7 0.6 %copy-done.4 = s32[1,1,256]{2,1,0:T(1,128)S(1)} copy-done((s32[1,1,256]{2,1,0:T(1,128)S(1)}, s32[1,1,256]{2,1,0:T(1,128)}, u32[]{:S(2)}) %copy-start.4) | copy-done | bytes 1048
  5.3 0.0 copy-done.3
  5.4 1.2 %spread_and_inner_rows.1 = (f32[8,5,2,8,256]{4,3,2,1,0:T(8,128)S(1)}, f32[3,2,2,32,128]{4,3,2,1,0:T(8,128)S(1)}) custom-call(s32[1,256]{1,0:T(1,128)S(1)} %bitcast.8, s32[1,256]{1,0:T(1,128)S(1)} %bitcast.9, f32[512,128]{1,0:T(8,128)S(1)} %bitcast.6, f32[256,128]{1,0:T(8,128)S(1)} %bitcast.7, f32[3,2,64,256]{3,2,1,0:T(8,128)S(1)} %pad_add_fusion.own_ref), custom_call_target="tpu_custom_call" | custom-call | flops 1000000000 | bytes 10000000 | tf_op jit(solution)/shard_map/spread_and_inner_rows/pallas_call | solution.py:226
  6.6 0.0 collective-permute-done.1.one_ref
  6.6 2.1 %collective-permute-done.two_ref = f32[3,2,8,256]{3,2,1,0:T(8,128)S(1)} collective-permute-done((f32[3,2,8,256]{3,2,1,0:T(8,128)S(1)}, f32[3,2,8,256]{3,2,1,0:T(8,128)S(1)}, u32[]{:S(2)}, u32[]{:S(2)}) %collective-permute-start) | collective-permute-done | bytes 49184 | tf_op jit(solution)/shard_map/ppermute | solution.py:223
  8.7 0.8 %end_rows.1 = f32[8,5,2,8,256]{4,3,2,1,0:T(8,128)S(1)} custom-call(s32[1]{0:T(128)} %bitcast.tile_ref, f32[3,2,2,32,128]{4,3,2,1,0:T(8,128)S(1)} %get-tuple-element.7.edge_ref, f32[3,2,8,256]{3,2,1,0:T(8,128)S(1)} %collective-permute-done.two_ref, f32[3,2,8,256]{3,2,1,0:T(8,128)S(1)} %collective-permute-done.1.one_ref, ...), custom_call_target="tpu_custom_call" | custom-call | flops 10000000 | bytes 1000000 | tf_op jit(solution)/shard_map/end_rows/pallas_call | solution.py:242
  9.5 0.0 copy-start
  9.5 14.8 %all_to_all.5.moved_ref = f32[8,5,2,8,256]{4,3,2,1,0:T(8,128)S(1)} all-to-all(f32[8,5,2,8,256]{4,3,2,1,0:T(8,128)S(1)} %end_rows.1), channel_id=1, replica_groups=mesh['sec'=8,'tile'=4] {'sec'}, dimensions={0} | all-to-all | bytes 1310720 | tf_op jit(solution)/shard_map/all_to_all | solution.py:252
  24.3 0.0 copy-done
  24.3 1.5 %cross_steps.1 = f32[2,16,8,256]{3,2,1,0:T(8,128)} custom-call(f32[8,5,2,8,256]{4,3,2,1,0:T(8,128)S(1)} %all_to_all.5.moved_ref, f32[16,8,256]{2,1,0:T(8,128)S(1)} %copy-done), custom_call_target="tpu_custom_call" | custom-call | flops 10000000 | bytes 800000 | tf_op jit(solution)/shard_map/cross_steps/pallas_call | solution.py:253
  (1 shorter events, 0.0 us)
Async XLA Ops:
  0.0 4.6 %copy-start.5 = (f32[2,2,64,256]{3,2,1,0:T(8,128)S(1)}, f32[2,2,64,256]{3,2,1,0:T(8,128)}, u32[]{:S(2)}) copy-start(f32[2,2,64,256]{3,2,1,0:T(8,128)} %param.7) | copy-start | bytes 786436
  0.0 4.6 %copy-start.6 = (f32[2,64,256]{2,1,0:T(8,128)S(1)}, f32[2,64,256]{2,1,0:T(8,128)}, u32[]{:S(2)}) copy-start(f32[2,64,256]{2,1,0:T(8,128)} %param.8) | copy-start | bytes 393220
  0.9 5.6 %collective-permute-start.1 = (f32[3,2,8,256]{3,2,1,0:T(8,128)S(1)}, f32[3,2,8,256]{3,2,1,0:T(8,128)S(1)}, u32[]{:S(2)}, u32[]{:S(2)}) collective-permute-start(f32[3,2,8,256]{3,2,1,0:T(8,128)S(1)} %get-tuple-element.9), channel_id=1, source_target_pairs={{0,1},{1,0},{2,3},{3,2},{4,5},{5,4},{6,7},{7,6},{8,9},{9,8},{10,11... | collective-permute-start | bytes 147464 | tf_op jit(solution)/shard_map/ppermute | solution.py:224
  2.6 2.1 %copy-start.1 = (f32[1,1,256,2,128]{4,3,2,1,0:T(2,128)S(1)}, f32[1,1,256,2,128]{4,3,2,1,0:T(2,128)}, u32[]{:S(2)}) copy-start(f32[1,1,256,2,128]{4,3,2,1,0:T(2,128)} %param.12) | copy-start | bytes 786436
  2.6 2.1 %copy-start.2 = (f32[1,1,256,128]{3,2,1,0:T(8,128)S(1)}, f32[1,1,256,128]{3,2,1,0:T(8,128)}, u32[]{:S(2)}) copy-start(f32[1,1,256,128]{3,2,1,0:T(8,128)} %param.13) | copy-start | bytes 393220
  2.6 6.1 %collective-permute-start = (f32[3,2,8,256]{3,2,1,0:T(8,128)S(1)}, f32[3,2,8,256]{3,2,1,0:T(8,128)S(1)}, u32[]{:S(2)}, u32[]{:S(2)}) collective-permute-start(f32[3,2,8,256]{3,2,1,0:T(8,128)S(1)} %get-tuple-element.10), channel_id=1, source_target_pairs={{0,0},{1,2},{2,1},{3,3},{4,4},{5,6},{6,5},{7,7},{8,8},{9,10},{10,9... | collective-permute-start | bytes 147464 | tf_op jit(solution)/shard_map/ppermute | solution.py:223
  4.7 0.7 %copy-start.4 = (s32[1,1,256]{2,1,0:T(1,128)S(1)}, s32[1,1,256]{2,1,0:T(1,128)}, u32[]{:S(2)}) copy-start(s32[1,1,256]{2,1,0:T(1,128)} %param.11) | copy-start | bytes 3076
  4.7 0.7 %copy-start.3 = (s32[1,1,256,1]{2,3,1,0:T(1,128)S(1)}, s32[1,1,256,1]{2,3,1,0:T(1,128)}, u32[]{:S(2)}) copy-start(s32[1,1,256,1]{2,3,1,0:T(1,128)} %param.10) | copy-start | bytes 3076
  9.5 14.8 %copy-start = (f32[16,8,256]{2,1,0:T(8,128)S(1)}, f32[16,8,256]{2,1,0:T(8,128)}, u32[]{:S(2)}) copy-start(f32[16,8,256]{2,1,0:T(8,128)} %stiff_ref.1) | copy-start | bytes 393220

commit v7 on v6

--- a/solution.py
+++ b/solution.py
@@ -130,7 +130,7 @@
     put_rows(held, out_ref, HALO, HALO, rows - HALO)
 
 
-def ends_kernel(tiles, tile_ref, edge_ref, two_ref, one_ref, mixed_ref, out_ref, held, *scratch):
+def ends_kernel(tiles, tile_ref, edge_ref, one_ref, two_ref, mixed_ref, out_ref, held, *scratch):
     blocks, width = held.shape[2], held.shape[-1]
     rows = out_ref.shape[0] * out_ref.shape[3]
     edge = HALO // out_ref.shape[3]
@@ -220,8 +220,8 @@
     own = jnp.pad(in_plane_force, ((0, 1),) + rest) + jnp.pad(stiffness[None], ((2, 0),) + rest)
 
     first, last = own[:, :, :HALO], own[:, :, rows - HALO :]
+    one = lax.ppermute(jnp.where(odd == 1, first, last), "tile", swaps[0])
     two = lax.ppermute(jnp.where(odd == 1, last, first), "tile", swaps[1])
-    one = lax.ppermute(jnp.where(odd == 1, first, last), "tile", swaps[0])
     mixed_shape = jax.ShapeDtypeStruct((groups, 5, layers, inner_rows, columns), jnp.float32)
     mixed, own_edges = pl.pallas_call(
         inner_kernel,
@@ -248,7 +248,7 @@
         compiler_params=LIMIT,
         cost_estimate=pl.CostEstimate(flops=10**7, bytes_accessed=10**6, transcendentals=0),
         name="end_rows",
-    )(tile.reshape(1), own_edges, two, one, mixed)
+    )(tile.reshape(1), own_edges, one, two, mixed)
     moved = lax.all_to_all(mixed, "sec", split_axis=0, concat_axis=0, tiled=True)
     return pl.pallas_call(
         cross_kernel,

time: 26 us -> 27 us (1.038)
  the two profiles are of different devices: /device:TPU:16 before, /device:TPU:0 now
where the time goes in v7:
time: 27 us; the launch traced here: 26.8 us
  blocking collectives  14.8 us (55%)
  starting transfers between devices  6.57 us (24%)
  Pallas kernels  3.5 us (13%)
  other arithmetic  0.97 us (4%)
  local copies, waits for them, and re-layouts  0.68 us (3%)
    all_to_all x1, blocking collectives, per_device(): lax.all_to_all(mixed, 'sec', split_axis=0, concat_axis=0, tiled=True)  14.8 us
    ppermute x1, starting transfers between devices, per_device(): one = lax.ppermute(jnp.where(odd == 1, first, last), 'tile', swaps[0])  5.91 us
    pallas_call x1, Pallas kernels, per_device(): pl.pallas_call(cross_kernel, out_shape=jax.ShapeDtypeStruct((2, groups *...  1.49 us
    pallas_call x1, Pallas kernels, per_device(): pl.pallas_call(inner_kernel, out_shape=[mixed_shape, jax.ShapeDtypeStruct...  1.18 us
    select_n x1, other arithmetic, per_device(): two = lax.ppermute(jnp.where(odd == 1, last, first), 'tile', swaps[1])  0.94 us
    pallas_call x1, Pallas kernels, per_device(): pl.pallas_call(functools.partial(ends_kernel, tiles), out_shape=mixed_sha...  0.82 us
    unnamed x14, local copies, waits for them, and re-layouts  0.68 us
    ppermute x1, starting transfers between devices, per_device(): two = lax.ppermute(jnp.where(odd == 1, last, first), 'tile', swaps[1])  0.66 us
  transfers between devices with their start and end apart: 2, of which 1 were waited for; matrix products, arithmetic and copies ran while one was open for 0% of the time, Pallas kernels for 4%

profile of v7, /device:TPU:0, one launch (start us, length us, event | category | flops | bytes accessed | tf_op | source)
XLA Modules:
  0.0 26.8 jit_solution(3293537452605021422)
XLA Ops:
  0.0 0.0 copy-start.5
  0.0 0.0 copy-start.6
  0.0 0.9 %broadcast_select_fusion = (f32[3,2,8,256]{3,2,1,0:T(8,128)S(1)}, f32[3,2,8,256]{3,2,1,0:T(8,128)S(1)}) fusion(pred[]{:T(512)S(6)} %eq.4, f32[1,2,64,256]{3,2,1,0:T(8,128)} %bitcast.10, f32[2,2,64,256]{3,2,1,0:T(8,128)} %param.7), kind=kLoop, calls=%fused_computation.7 | loop fusion | flops 73728 | bytes 491521 | tf_op jit(solution)/shard_map/jit(_where)/select_n | solution.py:224
  0.9 0.7 %collective-permute-start.1 = (f32[3,2,8,256]{3,2,1,0:T(8,128)S(1)}, f32[3,2,8,256]{3,2,1,0:T(8,128)S(1)}, u32[]{:S(2)}, u32[]{:S(2)}) collective-permute-start(f32[3,2,8,256]{3,2,1,0:T(8,128)S(1)} %get-tuple-element.9), channel_id=1, source_target_pairs={{0,0},{1,2},{2,1},{3,3},{4,4},{5,6},{6,5},{7,7},{8,8},{9,10},{10,9... | collective-permute-start | bytes 147464 | tf_op jit(solution)/shard_map/ppermute | solution.py:224
  1.6 0.0 copy-start.1
  1.6 0.0 copy-start.2
  1.6 5.9 %collective-permute-start = (f32[3,2,8,256]{3,2,1,0:T(8,128)S(1)}, f32[3,2,8,256]{3,2,1,0:T(8,128)S(1)}, u32[]{:S(2)}, u32[]{:S(2)}) collective-permute-start(f32[3,2,8,256]{3,2,1,0:T(8,128)S(1)} %get-tuple-element.10), channel_id=1, source_target_pairs={{0,1},{1,0},{2,3},{3,2},{4,5},{5,4},{6,7},{7,6},{8,9},{9,8},{10,11... | collective-permute-start | bytes 147464 | tf_op jit(solution)/shard_map/ppermute | solution.py:223
  7.6 0.0 copy-done.5
  7.6 0.0 copy-done.6
  7.6 0.0 copy-start.4
  7.6 0.0 copy-start.3
  7.6 0.0 copy-done.1
  7.6 0.0 copy-done.2
  7.6 0.6 %copy-done.4 = s32[1,1,256]{2,1,0:T(1,128)S(1)} copy-done((s32[1,1,256]{2,1,0:T(1,128)S(1)}, s32[1,1,256]{2,1,0:T(1,128)}, u32[]{:S(2)}) %copy-start.4) | copy-done | bytes 1048
  8.2 0.0 copy-done.3
  8.3 1.2 %spread_and_inner_rows.1 = (f32[8,5,2,8,256]{4,3,2,1,0:T(8,128)S(1)}, f32[3,2,2,32,128]{4,3,2,1,0:T(8,128)S(1)}) custom-call(s32[1,256]{1,0:T(1,128)S(1)} %bitcast.8, s32[1,256]{1,0:T(1,128)S(1)} %bitcast.9, f32[512,128]{1,0:T(8,128)S(1)} %bitcast.6, f32[256,128]{1,0:T(8,128)S(1)} %bitcast.7, f32[3,2,64,256]{3,2,1,0:T(8,128)S(1)} %pad_add_fusion.own_ref), custom_call_target="tpu_custom_call" | custom-call | flops 1000000000 | bytes 10000000 | tf_op jit(solution)/shard_map/spread_and_inner_rows/pallas_call | solution.py:226
  9.5 0.0 collective-permute-done.1.two_ref
  9.5 0.2 collective-permute-done.one_ref
  9.6 0.8 %end_rows.1 = f32[8,5,2,8,256]{4,3,2,1,0:T(8,128)S(1)} custom-call(s32[1]{0:T(128)} %bitcast.tile_ref, f32[3,2,2,32,128]{4,3,2,1,0:T(8,128)S(1)} %get-tuple-element.7.edge_ref, f32[3,2,8,256]{3,2,1,0:T(8,128)S(1)} %collective-permute-done.one_ref, f32[3,2,8,256]{3,2,1,0:T(8,128)S(1)} %collective-permute-done.1.two_ref, ...), custom_call_target="tpu_custom_call" | custom-call | flops 10000000 | bytes 1000000 | tf_op jit(solution)/shard_map/end_rows/pallas_call | solution.py:242
  10.4 0.0 copy-start
  10.5 14.8 %all_to_all.5.moved_ref = f32[8,5,2,8,256]{4,3,2,1,0:T(8,128)S(1)} all-to-all(f32[8,5,2,8,256]{4,3,2,1,0:T(8,128)S(1)} %end_rows.1), channel_id=1, replica_groups=mesh['sec'=8,'tile'=4] {'sec'}, dimensions={0} | all-to-all | bytes 1310720 | tf_op jit(solution)/shard_map/all_to_all | solution.py:252
  25.3 0.0 copy-done
  25.3 1.5 %cross_steps.1 = f32[2,16,8,256]{3,2,1,0:T(8,128)} custom-call(f32[8,5,2,8,256]{4,3,2,1,0:T(8,128)S(1)} %all_to_all.5.moved_ref, f32[16,8,256]{2,1,0:T(8,128)S(1)} %copy-done), custom_call_target="tpu_custom_call" | custom-call | flops 10000000 | bytes 800000 | tf_op jit(solution)/shard_map/cross_steps/pallas_call | solution.py:253
  (1 shorter events, 0.0 us)
Async XLA Ops:
  0.0 7.6 %copy-start.5 = (f32[2,2,64,256]{3,2,1,0:T(8,128)S(1)}, f32[2,2,64,256]{3,2,1,0:T(8,128)}, u32[]{:S(2)}) copy-start(f32[2,2,64,256]{3,2,1,0:T(8,128)} %param.7) | copy-start | bytes 786436
  0.0 7.6 %copy-start.6 = (f32[2,64,256]{2,1,0:T(8,128)S(1)}, f32[2,64,256]{2,1,0:T(8,128)}, u32[]{:S(2)}) copy-start(f32[2,64,256]{2,1,0:T(8,128)} %param.8) | copy-start | bytes 393220
  0.9 8.5 %collective-permute-start.1 = (f32[3,2,8,256]{3,2,1,0:T(8,128)S(1)}, f32[3,2,8,256]{3,2,1,0:T(8,128)S(1)}, u32[]{:S(2)}, u32[]{:S(2)}) collective-permute-start(f32[3,2,8,256]{3,2,1,0:T(8,128)S(1)} %get-tuple-element.9), channel_id=1, source_target_pairs={{0,0},{1,2},{2,1},{3,3},{4,4},{5,6},{6,5},{7,7},{8,8},{9,10},{10,9... | collective-permute-start | bytes 147464 | tf_op jit(solution)/shard_map/ppermute | solution.py:224
  1.6 6.0 %copy-start.1 = (f32[1,1,256,2,128]{4,3,2,1,0:T(2,128)S(1)}, f32[1,1,256,2,128]{4,3,2,1,0:T(2,128)}, u32[]{:S(2)}) copy-start(f32[1,1,256,2,128]{4,3,2,1,0:T(2,128)} %param.12) | copy-start | bytes 786436
  1.6 6.0 %copy-start.2 = (f32[1,1,256,128]{3,2,1,0:T(8,128)S(1)}, f32[1,1,256,128]{3,2,1,0:T(8,128)}, u32[]{:S(2)}) copy-start(f32[1,1,256,128]{3,2,1,0:T(8,128)} %param.13) | copy-start | bytes 393220
  1.6 8.0 %collective-permute-start = (f32[3,2,8,256]{3,2,1,0:T(8,128)S(1)}, f32[3,2,8,256]{3,2,1,0:T(8,128)S(1)}, u32[]{:S(2)}, u32[]{:S(2)}) collective-permute-start(f32[3,2,8,256]{3,2,1,0:T(8,128)S(1)} %get-tuple-element.10), channel_id=1, source_target_pairs={{0,1},{1,0},{2,3},{3,2},{4,5},{5,4},{6,7},{7,6},{8,9},{9,8},{10,11... | collective-permute-start | bytes 147464 | tf_op jit(solution)/shard_map/ppermute | solution.py:223
  7.6 0.7 %copy-start.4 = (s32[1,1,256]{2,1,0:T(1,128)S(1)}, s32[1,1,256]{2,1,0:T(1,128)}, u32[]{:S(2)}) copy-start(s32[1,1,256]{2,1,0:T(1,128)} %param.11) | copy-start | bytes 3076
  7.6 0.7 %copy-start.3 = (s32[1,1,256,1]{2,3,1,0:T(1,128)S(1)}, s32[1,1,256,1]{2,3,1,0:T(1,128)}, u32[]{:S(2)}) copy-start(s32[1,1,256,1]{2,3,1,0:T(1,128)} %param.10) | copy-start | bytes 3076
  10.4 14.8 %copy-start = (f32[16,8,256]{2,1,0:T(8,128)S(1)}, f32[16,8,256]{2,1,0:T(8,128)}, u32[]{:S(2)}) copy-start(f32[16,8,256]{2,1,0:T(8,128)} %stiff_ref.1) | copy-start | bytes 393220

commit v8 on v6

--- a/solution.py
+++ b/solution.py
@@ -130,23 +130,28 @@
     put_rows(held, out_ref, HALO, HALO, rows - HALO)
 
 
-def ends_kernel(tiles, tile_ref, edge_ref, two_ref, one_ref, mixed_ref, out_ref, held, *scratch):
-    blocks, width = held.shape[2], held.shape[-1]
-    rows = out_ref.shape[0] * out_ref.shape[3]
-    edge = HALO // out_ref.shape[3]
-    held[:, :, :, HALO : 5 * HALO] = edge_ref[...]
+def end_kernel(tiles, first_swap, tile_ref, edge_ref, halo_ref, mixed_ref, out_ref, held, *scratch):
+    _, layers, blocks, _, width = held.shape
+    groups, _, _, inner_rows, _ = out_ref.shape
+    count = HALO // inner_rows
     tile = tile_ref[0]
-    odd = (tile & 1) == 1
+    top = (tile & 1) == (1 if first_swap else 0)
+    alone = jnp.where(top, tile == 0, tile == tiles - 1)
     for b in range(blocks):
-        span = slice(b * width, (b + 1) * width)
-        one, two = one_ref[:, :, :, span], two_ref[:, :, :, span]
-        held[:, :, b, :HALO] = jnp.where(tile == 0, 0.0, jnp.where(odd, one, two))
-        held[:, :, b, 5 * HALO :] = jnp.where(tile == tiles - 1, 0.0, jnp.where(odd, two, one))
-    out_ref[:, 2:] = mixed_ref[:, 2:]
-    out_ref[edge:-edge, :2] = mixed_ref[edge:-edge, :2]
+        halo = jnp.where(alone, 0.0, halo_ref[:, :, :, b * width : (b + 1) * width])
+        own = [edge_ref[:, :, b, n * HALO : (n + 1) * HALO] for n in range(4)]
+        held[:, :, b, :HALO] = jnp.where(top, halo, own[2])
+        held[:, :, b, HALO : 2 * HALO] = jnp.where(top, own[0], own[3])
+        held[:, :, b, 2 * HALO :] = jnp.where(top, own[1], halo)
+    out_ref[...] = mixed_ref[...]
     relax(held, *scratch)
-    put_rows(held, out_ref, HALO, 0, HALO)
-    put_rows(held, out_ref, 4 * HALO, rows - HALO, rows)
+    at = jnp.where(top, 0, groups - count)
+    for c in range(2):
+        for l in range(layers):
+            for b in range(blocks):
+                for n in range(count):
+                    start = HALO + n * inner_rows
+                    out_ref[at + n, c, l, :, b * width : (b + 1) * width] = held[c, l, b, start : start + inner_rows, :]
 
 
 def relax_scratch(layers, blocks, total, width):
@@ -239,16 +244,17 @@
         patch_conf.reshape(count, width),
         own,
     )
-    mixed = pl.pallas_call(
-        functools.partial(ends_kernel, tiles),
-        out_shape=mixed_shape,
-        in_specs=[pl.BlockSpec(memory_space=pltpu.SMEM)] + [VMEM] * 4,
-        out_specs=VMEM,
-        scratch_shapes=relax_scratch(layers, blocks, 6 * HALO, width),
-        compiler_params=LIMIT,
-        cost_estimate=pl.CostEstimate(flops=10**7, bytes_accessed=10**6, transcendentals=0),
-        name="end_rows",
-    )(tile.reshape(1), own_edges, two, one, mixed)
+    for halo, first_swap in ((one, True), (two, False)):
+        mixed = pl.pallas_call(
+            functools.partial(end_kernel, tiles, first_swap),
+            out_shape=mixed_shape,
+            in_specs=[pl.BlockSpec(memory_space=pltpu.SMEM)] + [VMEM] * 3,
+            out_specs=VMEM,
+            scratch_shapes=relax_scratch(layers, blocks, 3 * HALO, width),
+            compiler_params=LIMIT,
+            cost_estimate=pl.CostEstimate(flops=10**7, bytes_accessed=10**6, transcendentals=0),
+            name="end_rows",
+        )(tile.reshape(1), own_edges, halo, mixed)
     moved = lax.all_to_all(mixed, "sec", split_axis=0, concat_axis=0, tiled=True)
     return pl.pallas_call(
         cross_kernel,

time: 26 us -> 25.9 us (level)
  the two profiles are of different devices: /device:TPU:16 before, /device:TPU:8 now
where the time goes in v8:
time: 25.9 us; the launch traced here: 25.7 us
  blocking collectives  14.8 us (57%)
  starting transfers between devices  5.22 us (20%)
  Pallas kernels  3.9 us (15%)
  other arithmetic  0.97 us (4%)
  local copies, waits for them, and re-layouts  0.68 us (3%)
    all_to_all x1, blocking collectives, per_device(): lax.all_to_all(mixed, 'sec', split_axis=0, concat_axis=0, tiled=True)  14.8 us
    ppermute x1, starting transfers between devices, per_device(): two = lax.ppermute(jnp.where(odd == 1, last, first), 'tile', swaps[1])  5.15 us
    pallas_call x1, Pallas kernels, per_device(): pl.pallas_call(cross_kernel, out_shape=jax.ShapeDtypeStruct((2, groups *...  1.49 us
    pallas_call x2, Pallas kernels, per_device(): pl.pallas_call(functools.partial(end_kernel, tiles, first_swap), out_shap...  1.22 us
    pallas_call x1, Pallas kernels, per_device(): pl.pallas_call(inner_kernel, out_shape=[mixed_shape, jax.ShapeDtypeStruct...  1.18 us
    select_n x1, other arithmetic, per_device(): one = lax.ppermute(jnp.where(odd == 1, first, last), 'tile', swaps[0])  0.94 us
    unnamed x14, local copies, waits for them, and re-layouts  0.68 us
  transfers between devices with their start and end apart: 2, of which 0 were waited for; matrix products, arithmetic and copies ran while one was open for 0% of the time, Pallas kernels for 7%

profile of v8, /device:TPU:8, one launch (start us, length us, event | category | flops | bytes accessed | tf_op | source)
XLA Modules:
  0.0 25.7 jit_solution(11516632161815603617)
XLA Ops:
  0.0 0.0 copy-start.5
  0.0 0.0 copy-start.6
  0.0 0.9 %broadcast_select_fusion = (f32[3,2,8,256]{3,2,1,0:T(8,128)S(1)}, f32[3,2,8,256]{3,2,1,0:T(8,128)S(1)}) fusion(pred[]{:T(512)S(6)} %eq.4, f32[1,2,64,256]{3,2,1,0:T(8,128)} %bitcast.10, f32[2,2,64,256]{3,2,1,0:T(8,128)} %param.7), kind=kLoop, calls=%fused_computation.7 | loop fusion | flops 73728 | bytes 491521 | tf_op jit(solution)/shard_map/jit(_where)/select_n | solution.py:229
  0.9 0.1 collective-permute-start.1
  1.0 0.0 copy-start.1
  1.0 0.0 copy-start.2
  1.0 5.1 %collective-permute-start = (f32[3,2,8,256]{3,2,1,0:T(8,128)S(1)}, f32[3,2,8,256]{3,2,1,0:T(8,128)S(1)}, u32[]{:S(2)}, u32[]{:S(2)}) collective-permute-start(f32[3,2,8,256]{3,2,1,0:T(8,128)S(1)} %get-tuple-element.10), channel_id=1, source_target_pairs={{0,0},{1,2},{2,1},{3,3},{4,4},{5,6},{6,5},{7,7},{8,8},{9,10},{10,9... | collective-permute-start | bytes 147464 | tf_op jit(solution)/shard_map/ppermute | solution.py:228
  6.2 0.0 copy-done.5
  6.2 0.0 copy-done.6
  6.2 0.0 copy-start.4
  6.3 0.0 copy-start.3
  6.3 0.0 copy-done.1
  6.3 0.0 copy-done.2
  6.3 0.6 %copy-done.4 = s32[1,1,256]{2,1,0:T(1,128)S(1)} copy-done((s32[1,1,256]{2,1,0:T(1,128)S(1)}, s32[1,1,256]{2,1,0:T(1,128)}, u32[]{:S(2)}) %copy-start.4) | copy-done | bytes 1048
  6.9 0.0 copy-done.3
  7.0 1.2 %spread_and_inner_rows.1 = (f32[8,5,2,8,256]{4,3,2,1,0:T(8,128)S(1)}, f32[3,2,2,32,128]{4,3,2,1,0:T(8,128)S(1)}) custom-call(s32[1,256]{1,0:T(1,128)S(1)} %bitcast.8, s32[1,256]{1,0:T(1,128)S(1)} %bitcast.9, f32[512,128]{1,0:T(8,128)S(1)} %bitcast.6, f32[256,128]{1,0:T(8,128)S(1)} %bitcast.7, f32[3,2,64,256]{3,2,1,0:T(8,128)S(1)} %pad_add_fusion.own_ref), custom_call_target="tpu_custom_call" | custom-call | flops 1000000000 | bytes 10000000 | tf_op jit(solution)/shard_map/spread_and_inner_rows/pallas_call | solution.py:231
  8.1 0.0 collective-permute-done.1.halo_ref
  8.1 0.6 %end_rows.2.mixed_ref = f32[8,5,2,8,256]{4,3,2,1,0:T(8,128)S(1)} custom-call(s32[1]{0:T(128)} %bitcast.tile_ref, f32[3,2,2,32,128]{4,3,2,1,0:T(8,128)S(1)} %get-tuple-element.7.edge_ref, f32[3,2,8,256]{3,2,1,0:T(8,128)S(1)} %collective-permute-done.1.halo_ref, f32[8,5,2,8,256]{4,3,2,1,0:T(8,128)S(1)} %get-tuple-element.8.mixed_ref), custom_call_target="tpu_custom_call" | custom-call | flops 10000000 | bytes 1000000 | tf_op jit(solution)/shard_map/end_rows/pallas_call | solution.py:248
  8.8 0.0 collective-permute-done.halo_ref
  8.8 0.6 %end_rows.3 = f32[8,5,2,8,256]{4,3,2,1,0:T(8,128)S(1)} custom-call(s32[1]{0:T(128)} %bitcast.tile_ref, f32[3,2,2,32,128]{4,3,2,1,0:T(8,128)S(1)} %get-tuple-element.7.edge_ref, f32[3,2,8,256]{3,2,1,0:T(8,128)S(1)} %collective-permute-done.halo_ref, f32[8,5,2,8,256]{4,3,2,1,0:T(8,128)S(1)} %end_rows.2.mixed_ref), custom_call_target="tpu_custom_call" | custom-call | flops 10000000 | bytes 1000000 | tf_op jit(solution)/shard_map/end_rows/pallas_call | solution.py:248
  9.4 0.0 copy-start
  9.4 14.8 %all_to_all.5.moved_ref = f32[8,5,2,8,256]{4,3,2,1,0:T(8,128)S(1)} all-to-all(f32[8,5,2,8,256]{4,3,2,1,0:T(8,128)S(1)} %end_rows.3), channel_id=1, replica_groups=mesh['sec'=8,'tile'=4] {'sec'}, dimensions={0} | all-to-all | bytes 1310720 | tf_op jit(solution)/shard_map/all_to_all | solution.py:258
  24.2 0.0 copy-done
  24.2 1.5 %cross_steps.1 = f32[2,16,8,256]{3,2,1,0:T(8,128)} custom-call(f32[8,5,2,8,256]{4,3,2,1,0:T(8,128)S(1)} %all_to_all.5.moved_ref, f32[16,8,256]{2,1,0:T(8,128)S(1)} %copy-done), custom_call_target="tpu_custom_call" | custom-call | flops 10000000 | bytes 800000 | tf_op jit(solution)/shard_map/cross_steps/pallas_call | solution.py:259
  (1 shorter events, 0.0 us)
Async XLA Ops:
  0.0 6.2 %copy-start.5 = (f32[2,2,64,256]{3,2,1,0:T(8,128)S(1)}, f32[2,2,64,256]{3,2,1,0:T(8,128)}, u32[]{:S(2)}) copy-start(f32[2,2,64,256]{3,2,1,0:T(8,128)} %param.7) | copy-start | bytes 786436
  0.0 6.2 %copy-start.6 = (f32[2,64,256]{2,1,0:T(8,128)S(1)}, f32[2,64,256]{2,1,0:T(8,128)}, u32[]{:S(2)}) copy-start(f32[2,64,256]{2,1,0:T(8,128)} %param.8) | copy-start | bytes 393220
  0.9 7.2 %collective-permute-start.1 = (f32[3,2,8,256]{3,2,1,0:T(8,128)S(1)}, f32[3,2,8,256]{3,2,1,0:T(8,128)S(1)}, u32[]{:S(2)}, u32[]{:S(2)}) collective-permute-start(f32[3,2,8,256]{3,2,1,0:T(8,128)S(1)} %get-tuple-element.9), channel_id=1, source_target_pairs={{0,1},{1,0},{2,3},{3,2},{4,5},{5,4},{6,7},{7,6},{8,9},{9,8},{10,11... | collective-permute-start | bytes 147464 | tf_op jit(solution)/shard_map/ppermute | solution.py:229
  1.0 5.3 %copy-start.1 = (f32[1,1,256,2,128]{4,3,2,1,0:T(2,128)S(1)}, f32[1,1,256,2,128]{4,3,2,1,0:T(2,128)}, u32[]{:S(2)}) copy-start(f32[1,1,256,2,128]{4,3,2,1,0:T(2,128)} %param.12) | copy-start | bytes 786436
  1.0 5.3 %copy-start.2 = (f32[1,1,256,128]{3,2,1,0:T(8,128)S(1)}, f32[1,1,256,128]{3,2,1,0:T(8,128)}, u32[]{:S(2)}) copy-start(f32[1,1,256,128]{3,2,1,0:T(8,128)} %param.13) | copy-start | bytes 393220
  1.0 7.7 %collective-permute-start = (f32[3,2,8,256]{3,2,1,0:T(8,128)S(1)}, f32[3,2,8,256]{3,2,1,0:T(8,128)S(1)}, u32[]{:S(2)}, u32[]{:S(2)}) collective-permute-start(f32[3,2,8,256]{3,2,1,0:T(8,128)S(1)} %get-tuple-element.10), channel_id=1, source_target_pairs={{0,0},{1,2},{2,1},{3,3},{4,4},{5,6},{6,5},{7,7},{8,8},{9,10},{10,9... | collective-permute-start | bytes 147464 | tf_op jit(solution)/shard_map/ppermute | solution.py:228
  6.2 0.7 %copy-start.4 = (s32[1,1,256]{2,1,0:T(1,128)S(1)}, s32[1,1,256]{2,1,0:T(1,128)}, u32[]{:S(2)}) copy-start(s32[1,1,256]{2,1,0:T(1,128)} %param.11) | copy-start | bytes 3076
  6.3 0.7 %copy-start.3 = (s32[1,1,256,1]{2,3,1,0:T(1,128)S(1)}, s32[1,1,256,1]{2,3,1,0:T(1,128)}, u32[]{:S(2)}) copy-start(s32[1,1,256,1]{2,3,1,0:T(1,128)} %param.10) | copy-start | bytes 3076
  9.4 14.8 %copy-start = (f32[16,8,256]{2,1,0:T(8,128)S(1)}, f32[16,8,256]{2,1,0:T(8,128)}, u32[]{:S(2)}) copy-start(f32[16,8,256]{2,1,0:T(8,128)} %stiff_ref.1) | copy-start | bytes 393220

commit v9 on v8

--- a/solution.py
+++ b/solution.py
@@ -177,8 +177,7 @@
         span = pl.ds(pl.multiple_of(b * width, width), width)
         return pltpu.make_async_copy(result.at[index], out_ref.at[c, :, :, span], sems.at[index])
 
-    def one(index, carry):
-        b, c = index // 2, index % 2
+    def one(b, carry):
         span = pl.ds(pl.multiple_of(b * width, width), width)
 
         def channel(c):
@@ -186,20 +185,25 @@
 
         spring = STEP_CROSS * stiff_ref[:, :, span]
         weight = STEP_CROSS * channel(4)
-        pull = STEP_CROSS * channel(2 + c)
-
-        def step(_, field):
-            rise = field - jnp.concatenate([zero, field[:-1]], axis=0)
-            rise_above = jnp.concatenate([rise[1:], -field[-1:]], axis=0)
-            stretch = pull - weight * rise
-            stretch_above = jnp.concatenate([stretch[1:], zero], axis=0)
-            return field + (spring * (rise_above - rise) + (stretch - stretch_above))
-
-        result[index] = lax.fori_loop(0, ZSTEPS, step, channel(c), unroll=True)
-        outgoing(index).start()
+        pulls = [STEP_CROSS * channel(2 + c) for c in range(2)]
+
+        def step(_, fields):
+            stepped = []
+            for field, pull in zip(fields, pulls):
+                rise = field - jnp.concatenate([zero, field[:-1]], axis=0)
+                rise_above = jnp.concatenate([rise[1:], -field[-1:]], axis=0)
+                stretch = pull - weight * rise
+                stretch_above = jnp.concatenate([stretch[1:], zero], axis=0)
+                stepped.append(field + (spring * (rise_above - rise) + (stretch - stretch_above)))
+            return stepped
+
+        fields = lax.fori_loop(0, ZSTEPS, step, [channel(c) for c in range(2)], unroll=True)
+        for c in range(2):
+            result[2 * b + c] = fields[c]
+            outgoing(2 * b + c).start()
         return carry
 
-    lax.fori_loop(0, 2 * blocks, one, 0)
+    lax.fori_loop(0, blocks, one, 0)
     for index in range(2 * blocks):
         outgoing(index).wait()
 

time: 25.9 us -> 25.8 us (level)
  no operation moved by 1% of the time
where the time goes in v9:
time: 25.8 us; the launch traced here: 25.6 us
  blocking collectives  14.8 us (57%)
  starting transfers between devices  5.22 us (20%)
  Pallas kernels  3.85 us (15%)
  other arithmetic  0.97 us (4%)
  local copies, waits for them, and re-layouts  0.68 us (3%)
    all_to_all x1, blocking collectives, per_device(): lax.all_to_all(mixed, 'sec', split_axis=0, concat_axis=0, tiled=True)  14.8 us
    ppermute x1, starting transfers between devices, per_device(): two = lax.ppermute(jnp.where(odd == 1, last, first), 'tile', swaps[1])  5.15 us
    pallas_call x1, Pallas kernels, per_device(): pl.pallas_call(cross_kernel, out_shape=jax.ShapeDtypeStruct((2, groups *...  1.44 us
    pallas_call x2, Pallas kernels, per_device(): pl.pallas_call(functools.partial(end_kernel, tiles, first_swap), out_shap...  1.22 us
    pallas_call x1, Pallas kernels, per_device(): pl.pallas_call(inner_kernel, out_shape=[mixed_shape, jax.ShapeDtypeStruct...  1.18 us
    select_n x1, other arithmetic, per_device(): one = lax.ppermute(jnp.where(odd == 1, first, last), 'tile', swaps[0])  0.94 us
    unnamed x14, local copies, waits for them, and re-layouts  0.68 us
  transfers between devices with their start and end apart: 2, of which 0 were waited for; matrix products, arithmetic and copies ran while one was open for 0% of the time, Pallas kernels for 7%

profile of v9, /device:TPU:8, one launch (start us, length us, event | category | flops | bytes accessed | tf_op | source)
XLA Modules:
  0.0 25.6 jit_solution(12753113029283900391)
XLA Ops:
  0.0 0.0 copy-start.5
  0.0 0.0 copy-start.6
  0.0 0.9 %broadcast_select_fusion = (f32[3,2,8,256]{3,2,1,0:T(8,128)S(1)}, f32[3,2,8,256]{3,2,1,0:T(8,128)S(1)}) fusion(pred[]{:T(512)S(6)} %eq.4, f32[1,2,64,256]{3,2,1,0:T(8,128)} %bitcast.10, f32[2,2,64,256]{3,2,1,0:T(8,128)} %param.7), kind=kLoop, calls=%fused_computation.7 | loop fusion | flops 73728 | bytes 491521 | tf_op jit(solution)/shard_map/jit(_where)/select_n | solution.py:233
  0.9 0.1 collective-permute-start.1
  1.0 0.0 copy-start.1
  1.0 0.0 copy-start.2
  1.0 5.1 %collective-permute-start = (f32[3,2,8,256]{3,2,1,0:T(8,128)S(1)}, f32[3,2,8,256]{3,2,1,0:T(8,128)S(1)}, u32[]{:S(2)}, u32[]{:S(2)}) collective-permute-start(f32[3,2,8,256]{3,2,1,0:T(8,128)S(1)} %get-tuple-element.10), channel_id=1, source_target_pairs={{0,0},{1,2},{2,1},{3,3},{4,4},{5,6},{6,5},{7,7},{8,8},{9,10},{10,9... | collective-permute-start | bytes 147464 | tf_op jit(solution)/shard_map/ppermute | solution.py:232
  6.2 0.0 copy-done.5
  6.2 0.0 copy-done.6
  6.2 0.0 copy-start.4
  6.3 0.0 copy-start.3
  6.3 0.0 copy-done.1
  6.3 0.0 copy-done.2
  6.3 0.6 %copy-done.4 = s32[1,1,256]{2,1,0:T(1,128)S(1)} copy-done((s32[1,1,256]{2,1,0:T(1,128)S(1)}, s32[1,1,256]{2,1,0:T(1,128)}, u32[]{:S(2)}) %copy-start.4) | copy-done | bytes 1048
  6.9 0.0 copy-done.3
  7.0 1.2 %spread_and_inner_rows.1 = (f32[8,5,2,8,256]{4,3,2,1,0:T(8,128)S(1)}, f32[3,2,2,32,128]{4,3,2,1,0:T(8,128)S(1)}) custom-call(s32[1,256]{1,0:T(1,128)S(1)} %bitcast.8, s32[1,256]{1,0:T(1,128)S(1)} %bitcast.9, f32[512,128]{1,0:T(8,128)S(1)} %bitcast.6, f32[256,128]{1,0:T(8,128)S(1)} %bitcast.7, f32[3,2,64,256]{3,2,1,0:T(8,128)S(1)} %pad_add_fusion.own_ref), custom_call_target="tpu_custom_call" | custom-call | flops 1000000000 | bytes 10000000 | tf_op jit(solution)/shard_map/spread_and_inner_rows/pallas_call | solution.py:235
  8.1 0.0 collective-permute-done.1.halo_ref
  8.1 0.6 %end_rows.2.mixed_ref = f32[8,5,2,8,256]{4,3,2,1,0:T(8,128)S(1)} custom-call(s32[1]{0:T(128)} %bitcast.tile_ref, f32[3,2,2,32,128]{4,3,2,1,0:T(8,128)S(1)} %get-tuple-element.7.edge_ref, f32[3,2,8,256]{3,2,1,0:T(8,128)S(1)} %collective-permute-done.1.halo_ref, f32[8,5,2,8,256]{4,3,2,1,0:T(8,128)S(1)} %get-tuple-element.8.mixed_ref), custom_call_target="tpu_custom_call" | custom-call | flops 10000000 | bytes 1000000 | tf_op jit(solution)/shard_map/end_rows/pallas_call | solution.py:252
  8.8 0.0 collective-permute-done.halo_ref
  8.8 0.6 %end_rows.3 = f32[8,5,2,8,256]{4,3,2,1,0:T(8,128)S(1)} custom-call(s32[1]{0:T(128)} %bitcast.tile_ref, f32[3,2,2,32,128]{4,3,2,1,0:T(8,128)S(1)} %get-tuple-element.7.edge_ref, f32[3,2,8,256]{3,2,1,0:T(8,128)S(1)} %collective-permute-done.halo_ref, f32[8,5,2,8,256]{4,3,2,1,0:T(8,128)S(1)} %end_rows.2.mixed_ref), custom_call_target="tpu_custom_call" | custom-call | flops 10000000 | bytes 1000000 | tf_op jit(solution)/shard_map/end_rows/pallas_call | solution.py:252
  9.4 0.0 copy-start
  9.4 14.8 %all_to_all.5.moved_ref = f32[8,5,2,8,256]{4,3,2,1,0:T(8,128)S(1)} all-to-all(f32[8,5,2,8,256]{4,3,2,1,0:T(8,128)S(1)} %end_rows.3), channel_id=1, replica_groups=mesh['sec'=8,'tile'=4] {'sec'}, dimensions={0} | all-to-all | bytes 1310720 | tf_op jit(solution)/shard_map/all_to_all | solution.py:262
  24.2 0.0 copy-done
  24.2 1.4 %cross_steps.1 = f32[2,16,8,256]{3,2,1,0:T(8,128)} custom-call(f32[8,5,2,8,256]{4,3,2,1,0:T(8,128)S(1)} %all_to_all.5.moved_ref, f32[16,8,256]{2,1,0:T(8,128)S(1)} %copy-done), custom_call_target="tpu_custom_call" | custom-call | flops 10000000 | bytes 800000 | tf_op jit(solution)/shard_map/cross_steps/pallas_call | solution.py:263
  (1 shorter events, 0.0 us)
Async XLA Ops:
  0.0 6.2 %copy-start.5 = (f32[2,2,64,256]{3,2,1,0:T(8,128)S(1)}, f32[2,2,64,256]{3,2,1,0:T(8,128)}, u32[]{:S(2)}) copy-start(f32[2,2,64,256]{3,2,1,0:T(8,128)} %param.7) | copy-start | bytes 786436
  0.0 6.2 %copy-start.6 = (f32[2,64,256]{2,1,0:T(8,128)S(1)}, f32[2,64,256]{2,1,0:T(8,128)}, u32[]{:S(2)}) copy-start(f32[2,64,256]{2,1,0:T(8,128)} %param.8) | copy-start | bytes 393220
  0.9 7.2 %collective-permute-start.1 = (f32[3,2,8,256]{3,2,1,0:T(8,128)S(1)}, f32[3,2,8,256]{3,2,1,0:T(8,128)S(1)}, u32[]{:S(2)}, u32[]{:S(2)}) collective-permute-start(f32[3,2,8,256]{3,2,1,0:T(8,128)S(1)} %get-tuple-element.9), channel_id=1, source_target_pairs={{0,1},{1,0},{2,3},{3,2},{4,5},{5,4},{6,7},{7,6},{8,9},{9,8},{10,11... | collective-permute-start | bytes 147464 | tf_op jit(solution)/shard_map/ppermute | solution.py:233
  1.0 5.3 %copy-start.1 = (f32[1,1,256,2,128]{4,3,2,1,0:T(2,128)S(1)}, f32[1,1,256,2,128]{4,3,2,1,0:T(2,128)}, u32[]{:S(2)}) copy-start(f32[1,1,256,2,128]{4,3,2,1,0:T(2,128)} %param.12) | copy-start | bytes 786436
  1.0 5.3 %copy-start.2 = (f32[1,1,256,128]{3,2,1,0:T(8,128)S(1)}, f32[1,1,256,128]{3,2,1,0:T(8,128)}, u32[]{:S(2)}) copy-start(f32[1,1,256,128]{3,2,1,0:T(8,128)} %param.13) | copy-start | bytes 393220
  1.0 7.7 %collective-permute-start = (f32[3,2,8,256]{3,2,1,0:T(8,128)S(1)}, f32[3,2,8,256]{3,2,1,0:T(8,128)S(1)}, u32[]{:S(2)}, u32[]{:S(2)}) collective-permute-start(f32[3,2,8,256]{3,2,1,0:T(8,128)S(1)} %get-tuple-element.10), channel_id=1, source_target_pairs={{0,0},{1,2},{2,1},{3,3},{4,4},{5,6},{6,5},{7,7},{8,8},{9,10},{10,9... | collective-permute-start | bytes 147464 | tf_op jit(solution)/shard_map/ppermute | solution.py:232
  6.2 0.7 %copy-start.4 = (s32[1,1,256]{2,1,0:T(1,128)S(1)}, s32[1,1,256]{2,1,0:T(1,128)}, u32[]{:S(2)}) copy-start(s32[1,1,256]{2,1,0:T(1,128)} %param.11) | copy-start | bytes 3076
  6.3 0.7 %copy-start.3 = (s32[1,1,256,1]{2,3,1,0:T(1,128)S(1)}, s32[1,1,256,1]{2,3,1,0:T(1,128)}, u32[]{:S(2)}) copy-start(s32[1,1,256,1]{2,3,1,0:T(1,128)} %param.10) | copy-start | bytes 3076
  9.4 14.8 %copy-start = (f32[16,8,256]{2,1,0:T(8,128)S(1)}, f32[16,8,256]{2,1,0:T(8,128)}, u32[]{:S(2)}) copy-start(f32[16,8,256]{2,1,0:T(8,128)} %stiff_ref.1) | copy-start | bytes 393220

commit v10 on v9

--- a/solution.py
+++ b/solution.py
@@ -203,7 +203,7 @@
             outgoing(2 * b + c).start()
         return carry
 
-    lax.fori_loop(0, blocks, one, 0)
+    lax.fori_loop(0, blocks, one, 0, unroll=True)
     for index in range(2 * blocks):
         outgoing(index).wait()
 

time: 25.8 us -> 25.8 us (level)
  no operation moved by 1% of the time
where the time goes in v10:
time: 25.8 us; the launch traced here: 25.6 us
  blocking collectives  14.8 us (57%)
  starting transfers between devices  5.22 us (20%)
  Pallas kernels  3.83 us (15%)
  other arithmetic  0.97 us (4%)
  local copies, waits for them, and re-layouts  0.68 us (3%)
    all_to_all x1, blocking collectives, per_device(): lax.all_to_all(mixed, 'sec', split_axis=0, concat_axis=0, tiled=True)  14.8 us
    ppermute x1, starting transfers between devices, per_device(): two = lax.ppermute(jnp.where(odd == 1, last, first), 'tile', swaps[1])  5.15 us
    pallas_call x1, Pallas kernels, per_device(): pl.pallas_call(cross_kernel, out_shape=jax.ShapeDtypeStruct((2, groups *...  1.43 us
    pallas_call x2, Pallas kernels, per_device(): pl.pallas_call(functools.partial(end_kernel, tiles, first_swap), out_shap...  1.22 us
    pallas_call x1, Pallas kernels, per_device(): pl.pallas_call(inner_kernel, out_shape=[mixed_shape, jax.ShapeDtypeStruct...  1.18 us
    select_n x1, other arithmetic, per_device(): one = lax.ppermute(jnp.where(odd == 1, first, last), 'tile', swaps[0])  0.94 us
    unnamed x14, local copies, waits for them, and re-layouts  0.68 us
  transfers between devices with their start and end apart: 2, of which 0 were waited for; matrix products, arithmetic and copies ran while one was open for 0% of the time, Pallas kernels for 7%

profile of v10, /device:TPU:8, one launch (start us, length us, event | category | flops | bytes accessed | tf_op | source)
XLA Modules:
  0.0 25.6 jit_solution(2303880646979141132)
XLA Ops:
  0.0 0.0 copy-start.5
  0.0 0.0 copy-start.6
  0.0 0.9 %broadcast_select_fusion = (f32[3,2,8,256]{3,2,1,0:T(8,128)S(1)}, f32[3,2,8,256]{3,2,1,0:T(8,128)S(1)}) fusion(pred[]{:T(512)S(6)} %eq.4, f32[1,2,64,256]{3,2,1,0:T(8,128)} %bitcast.10, f32[2,2,64,256]{3,2,1,0:T(8,128)} %param.7), kind=kLoop, calls=%fused_computation.7 | loop fusion | flops 73728 | bytes 491521 | tf_op jit(solution)/shard_map/jit(_where)/select_n | solution.py:233
  0.9 0.1 collective-permute-start.1
  1.0 0.0 copy-start.1
  1.0 0.0 copy-start.2
  1.0 5.1 %collective-permute-start = (f32[3,2,8,256]{3,2,1,0:T(8,128)S(1)}, f32[3,2,8,256]{3,2,1,0:T(8,128)S(1)}, u32[]{:S(2)}, u32[]{:S(2)}) collective-permute-start(f32[3,2,8,256]{3,2,1,0:T(8,128)S(1)} %get-tuple-element.10), channel_id=1, source_target_pairs={{0,0},{1,2},{2,1},{3,3},{4,4},{5,6},{6,5},{7,7},{8,8},{9,10},{10,9... | collective-permute-start | bytes 147464 | tf_op jit(solution)/shard_map/ppermute | solution.py:232
  6.2 0.0 copy-done.5
  6.2 0.0 copy-done.6
  6.2 0.0 copy-start.4
  6.3 0.0 copy-start.3
  6.3 0.0 copy-done.1
  6.3 0.0 copy-done.2
  6.3 0.6 %copy-done.4 = s32[1,1,256]{2,1,0:T(1,128)S(1)} copy-done((s32[1,1,256]{2,1,0:T(1,128)S(1)}, s32[1,1,256]{2,1,0:T(1,128)}, u32[]{:S(2)}) %copy-start.4) | copy-done | bytes 1048
  6.9 0.0 copy-done.3
  7.0 1.2 %spread_and_inner_rows.1 = (f32[8,5,2,8,256]{4,3,2,1,0:T(8,128)S(1)}, f32[3,2,2,32,128]{4,3,2,1,0:T(8,128)S(1)}) custom-call(s32[1,256]{1,0:T(1,128)S(1)} %bitcast.8, s32[1,256]{1,0:T(1,128)S(1)} %bitcast.9, f32[512,128]{1,0:T(8,128)S(1)} %bitcast.6, f32[256,128]{1,0:T(8,128)S(1)} %bitcast.7, f32[3,2,64,256]{3,2,1,0:T(8,128)S(1)} %pad_add_fusion.own_ref), custom_call_target="tpu_custom_call" | custom-call | flops 1000000000 | bytes 10000000 | tf_op jit(solution)/shard_map/spread_and_inner_rows/pallas_call | solution.py:235
  8.1 0.0 collective-permute-done.1.halo_ref
  8.1 0.6 %end_rows.2.mixed_ref = f32[8,5,2,8,256]{4,3,2,1,0:T(8,128)S(1)} custom-call(s32[1]{0:T(128)} %bitcast.tile_ref, f32[3,2,2,32,128]{4,3,2,1,0:T(8,128)S(1)} %get-tuple-element.7.edge_ref, f32[3,2,8,256]{3,2,1,0:T(8,128)S(1)} %collective-permute-done.1.halo_ref, f32[8,5,2,8,256]{4,3,2,1,0:T(8,128)S(1)} %get-tuple-element.8.mixed_ref), custom_call_target="tpu_custom_call" | custom-call | flops 10000000 | bytes 1000000 | tf_op jit(solution)/shard_map/end_rows/pallas_call | solution.py:252
  8.8 0.0 collective-permute-done.halo_ref
  8.8 0.6 %end_rows.3 = f32[8,5,2,8,256]{4,3,2,1,0:T(8,128)S(1)} custom-call(s32[1]{0:T(128)} %bitcast.tile_ref, f32[3,2,2,32,128]{4,3,2,1,0:T(8,128)S(1)} %get-tuple-element.7.edge_ref, f32[3,2,8,256]{3,2,1,0:T(8,128)S(1)} %collective-permute-done.halo_ref, f32[8,5,2,8,256]{4,3,2,1,0:T(8,128)S(1)} %end_rows.2.mixed_ref), custom_call_target="tpu_custom_call" | custom-call | flops 10000000 | bytes 1000000 | tf_op jit(solution)/shard_map/end_rows/pallas_call | solution.py:252
  9.4 0.0 copy-start
  9.4 14.8 %all_to_all.5.moved_ref = f32[8,5,2,8,256]{4,3,2,1,0:T(8,128)S(1)} all-to-all(f32[8,5,2,8,256]{4,3,2,1,0:T(8,128)S(1)} %end_rows.3), channel_id=1, replica_groups=mesh['sec'=8,'tile'=4] {'sec'}, dimensions={0} | all-to-all | bytes 1310720 | tf_op jit(solution)/shard_map/all_to_all | solution.py:262
  24.2 0.0 copy-done
  24.2 1.4 %cross_steps.1 = f32[2,16,8,256]{3,2,1,0:T(8,128)} custom-call(f32[8,5,2,8,256]{4,3,2,1,0:T(8,128)S(1)} %all_to_all.5.moved_ref, f32[16,8,256]{2,1,0:T(8,128)S(1)} %copy-done), custom_call_target="tpu_custom_call" | custom-call | flops 10000000 | bytes 800000 | tf_op jit(solution)/shard_map/cross_steps/pallas_call | solution.py:263
  (1 shorter events, 0.0 us)
Async XLA Ops:
  0.0 6.2 %copy-start.5 = (f32[2,2,64,256]{3,2,1,0:T(8,128)S(1)}, f32[2,2,64,256]{3,2,1,0:T(8,128)}, u32[]{:S(2)}) copy-start(f32[2,2,64,256]{3,2,1,0:T(8,128)} %param.7) | copy-start | bytes 786436
  0.0 6.2 %copy-start.6 = (f32[2,64,256]{2,1,0:T(8,128)S(1)}, f32[2,64,256]{2,1,0:T(8,128)}, u32[]{:S(2)}) copy-start(f32[2,64,256]{2,1,0:T(8,128)} %param.8) | copy-start | bytes 393220
  0.9 7.2 %collective-permute-start.1 = (f32[3,2,8,256]{3,2,1,0:T(8,128)S(1)}, f32[3,2,8,256]{3,2,1,0:T(8,128)S(1)}, u32[]{:S(2)}, u32[]{:S(2)}) collective-permute-start(f32[3,2,8,256]{3,2,1,0:T(8,128)S(1)} %get-tuple-element.9), channel_id=1, source_target_pairs={{0,1},{1,0},{2,3},{3,2},{4,5},{5,4},{6,7},{7,6},{8,9},{9,8},{10,11... | collective-permute-start | bytes 147464 | tf_op jit(solution)/shard_map/ppermute | solution.py:233
  1.0 5.3 %copy-start.1 = (f32[1,1,256,2,128]{4,3,2,1,0:T(2,128)S(1)}, f32[1,1,256,2,128]{4,3,2,1,0:T(2,128)}, u32[]{:S(2)}) copy-start(f32[1,1,256,2,128]{4,3,2,1,0:T(2,128)} %param.12) | copy-start | bytes 786436
  1.0 5.3 %copy-start.2 = (f32[1,1,256,128]{3,2,1,0:T(8,128)S(1)}, f32[1,1,256,128]{3,2,1,0:T(8,128)}, u32[]{:S(2)}) copy-start(f32[1,1,256,128]{3,2,1,0:T(8,128)} %param.13) | copy-start | bytes 393220
  1.0 7.7 %collective-permute-start = (f32[3,2,8,256]{3,2,1,0:T(8,128)S(1)}, f32[3,2,8,256]{3,2,1,0:T(8,128)S(1)}, u32[]{:S(2)}, u32[]{:S(2)}) collective-permute-start(f32[3,2,8,256]{3,2,1,0:T(8,128)S(1)} %get-tuple-element.10), channel_id=1, source_target_pairs={{0,0},{1,2},{2,1},{3,3},{4,4},{5,6},{6,5},{7,7},{8,8},{9,10},{10,9... | collective-permute-start | bytes 147464 | tf_op jit(solution)/shard_map/ppermute | solution.py:232
  6.2 0.7 %copy-start.4 = (s32[1,1,256]{2,1,0:T(1,128)S(1)}, s32[1,1,256]{2,1,0:T(1,128)}, u32[]{:S(2)}) copy-start(s32[1,1,256]{2,1,0:T(1,128)} %param.11) | copy-start | bytes 3076
  6.3 0.7 %copy-start.3 = (s32[1,1,256,1]{2,3,1,0:T(1,128)S(1)}, s32[1,1,256,1]{2,3,1,0:T(1,128)}, u32[]{:S(2)}) copy-start(s32[1,1,256,1]{2,3,1,0:T(1,128)} %param.10) | copy-start | bytes 3076
  9.4 14.8 %copy-start = (f32[16,8,256]{2,1,0:T(8,128)S(1)}, f32[16,8,256]{2,1,0:T(8,128)}, u32[]{:S(2)}) copy-start(f32[16,8,256]{2,1,0:T(8,128)} %stiff_ref.1) | copy-start | bytes 393220
